TPU v7x, 512 devices: a whole 4x4x16 slice. The times are simulated.
512 devices in a mesh: row: 16 (over x, y), col: 32 (over z, core).
Axes of the slice: x: 4, y: 4, z: 16, core: 2. Of those that a mesh axis runs over, the one named last changes fastest.
Arguments:
- frames: bfloat16 [131072, 440], P(('row', 'col')), may hold values from -7 to 7
- labels: bfloat16 [131072, 147], P(('row', 'col')), may hold values from -6 to 6
- weights: float32 [131072, 147], P(('row', 'col')), may hold values from -0.0625 to 0.0625
- picks: int32 [2, 512], replicated, may hold values from 0 to 255, as said below
Outputs:
- updated: float32 [131072, 147], P(('row', 'col'))
Inputs may be any that keep to these rules, and one draw needn't show every extreme that they name: `picks`: device d owns the 1 block positions j with j == d; within one step, the frame indices at one device's positions are all different.
All inputs are finite; a program needn't handle non-finite values.
Results may differ from a plain program's by a relative error of at most 0.0005.
Values may be sent and summed in bfloat16 or wider, within the bound.
No kernel may reach another device: no remote copies, remote signals or barrier semaphores. Data moves between devices by JAX's collectives and lax.ppermute only.
A program may use at most 64 MiB of HBM per device.

v0:
```python
import jax
import jax.numpy as jnp
from jax import lax
from jax.sharding import PartitionSpec as P

STEPS = 2


ridge = 1.0


def kernel_of(first_rows, second_rows):
    inner_products = lax.dot_general(
        first_rows, second_rows, (((1,), (1,)), ((), ())), preferred_element_type=jnp.float32
    )
    first_wide = first_rows.astype(jnp.float32)
    second_wide = second_rows.astype(jnp.float32)
    first_sq = jnp.sum(first_wide * first_wide, axis=1)
    second_sq = jnp.sum(second_wide * second_wide, axis=1)
    width = first_rows.shape[1]
    return jnp.exp(-(first_sq[:, None] + second_sq[None, :] - 2.0 * inner_products) * (0.5 / width))


def contract(kernel_rows, weight_rows):
    return lax.dot_general(
        kernel_rows,
        weight_rows,
        (((0,), (0,)), ((), ())),
        precision=lax.Precision.HIGHEST,
        preferred_element_type=jnp.float32,
    )


def solve_block(gram, rhs):
    factor = jnp.linalg.cholesky(gram)
    middle = lax.linalg.triangular_solve(factor, rhs, left_side=True, lower=True)
    return lax.linalg.triangular_solve(factor, middle, left_side=True, lower=True, transpose_a=True)


def shards(frames, labels, weights, picks):
    devices = lax.axis_size(("row", "col"))
    block_len = picks.shape[1]
    per_device = block_len // devices
    targets = weights.shape[1]
    offset = lax.axis_index(("row", "col")) * per_device
    identity = jnp.eye(block_len, dtype=jnp.float32)
    current = weights
    for iteration in range(STEPS):
        local_pick = lax.dynamic_slice_in_dim(picks[iteration], offset, per_device, 0)
        block_frames = lax.all_gather(frames[local_pick], ("row", "col"), axis=0, tiled=True)
        near_kernel = kernel_of(frames, block_frames)
        mine = labels[local_pick].astype(jnp.float32) - ridge * current[local_pick]
        term = lax.dynamic_update_slice_in_dim(
            jnp.zeros((block_len, targets), jnp.float32), mine, offset, 0
        ) - contract(near_kernel, current)
        rhs = lax.psum(term, ("row", "col"))
        gram = kernel_of(block_frames, block_frames)
        delta = solve_block(gram + ridge * identity, rhs)
        current = current.at[local_pick].add(lax.dynamic_slice_in_dim(delta, offset, per_device, 0))
    return current


def solution(mesh):
    placed = (P(("row", "col"), None), P(("row", "col"), None), P(("row", "col"), None), P())
    return jax.shard_map(
        shards, mesh=mesh, in_specs=placed, out_specs=P(("row", "col"), None), check_vma=False
    )
```

profile of v0, /device:TPU:1, one launch (start us, length us, event | category | flops | bytes accessed | tf_op | source)
XLA Modules:
  0.0 1095.3 jit_solution(12703346124000410976)
XLA Ops:
  13.3 141.6 %all-gather = bf16[512,1,440]{2,1,0:T(2,128)(2,1)S(1)} all-gather(bf16[1,1,440]{2,1,0:T(2,128)(2,1)S(1)} %reshape.307), channel_id=1, replica_groups=mesh['row'=16,'col'=32] {'row','col'}, dimensions={0}, use_global_device_ids=true | all-gather | bytes 451440 | tf_op jit(solution)/shard_map/all_gather | solution.py:50
  157.4 1.4 convolution_subtract_fusion.1
  160.4 11.7 %cholesky.286 = f32[128,128]{1,0:T(8,128)S(1)} custom-call(f32[128,128]{1,0:T(8,128)S(1)} %cholesky.426), custom_call_target="Cholesky" | custom-call | tf_op jit(solution)/shard_map/jit(cholesky)/cholesky | solution.py:35
  172.3 9.8 custom-call.31
  182.8 11.7 %cholesky.305 = f32[128,128]{1,0:T(8,128)S(1)} custom-call(f32[128,128]{1,0:T(8,128)S(1)} %cholesky.430), custom_call_target="Cholesky" | custom-call | tf_op jit(solution)/shard_map/jit(cholesky)/cholesky | solution.py:35
  194.5 10.4 custom-call.32
  205.6 11.7 %cholesky.326 = f32[128,128]{1,0:T(8,128)S(1)} custom-call(f32[128,128]{1,0:T(8,128)S(1)} %cholesky.435), custom_call_target="Cholesky" | custom-call | tf_op jit(solution)/shard_map/jit(cholesky)/cholesky | solution.py:35
  217.3 9.8 custom-call.33
  227.7 11.8 %cholesky.343 = f32[128,128]{1,0:T(8,128)S(1)} custom-call(f32[128,128]{1,0:T(8,128)S(1)} %convolution_subtract_fusion.19), custom_call_target="Cholesky" | custom-call | tf_op jit(solution)/shard_map/jit(cholesky)/cholesky | solution.py:35
  244.8 7.5 while.16
  251.0 1.3 bitcast_dynamic-update-slice_fusion.4
  253.1 130.2 %all-gather.1 = bf16[512,1,440]{2,1,0:T(2,128)(2,1)S(1)} all-gather(bf16[1,1,440]{2,1,0:T(2,128)(2,1)S(1)} %reshape.309), channel_id=1, replica_groups=mesh['row'=16,'col'=32] {'row','col'}, dimensions={0}, use_global_device_ids=true | all-gather | bytes 451440 | tf_op jit(solution)/shard_map/all_gather | solution.py:50
  387.0 11.7 %cholesky.358 = f32[128,128]{1,0:T(8,128)S(1)} custom-call(f32[128,128]{1,0:T(8,128)S(1)} %cholesky.439), custom_call_target="Cholesky" | custom-call | tf_op jit(solution)/shard_map/jit(cholesky)/cholesky | solution.py:35
  400.9 11.3 %custom-call.36 = f32[1,128,128]{1,2,0:T(8,128)} custom-call(f32[1,128,128]{2,1,0:T(8,128)} %get-tuple-element.163), custom_call_target="InvertDiagBlocksLowerTriangular" | custom-call | tf_op jit(solution)/shard_map/jit(cholesky)/cholesky | solution.py:35
  415.0 13.2 %cholesky.377 = f32[128,128]{1,0:T(8,128)} custom-call(f32[128,128]{1,0:T(8,128)} %cholesky.443), custom_call_target="Cholesky" | custom-call | tf_op jit(solution)/shard_map/jit(cholesky)/cholesky | solution.py:35
  428.2 1.5 select_reduce_fusion.2
  429.7 11.4 %custom-call.37 = f32[1,128,128]{1,2,0:T(8,128)} custom-call(f32[1,128,128]{2,1,0:T(8,128)} %get-tuple-element.160), custom_call_target="InvertDiagBlocksLowerTriangular" | custom-call | tf_op jit(solution)/shard_map/jit(cholesky)/cholesky | solution.py:35
  444.0 13.2 %cholesky.398 = f32[128,128]{1,0:T(8,128)} custom-call(f32[128,128]{1,0:T(8,128)} %cholesky.448), custom_call_target="Cholesky" | custom-call | tf_op jit(solution)/shard_map/jit(cholesky)/cholesky | solution.py:35
  457.1 1.5 select_reduce_fusion.1
  458.6 11.3 %custom-call.38 = f32[1,128,128]{1,2,0:T(8,128)} custom-call(f32[1,128,128]{2,1,0:T(8,128)} %get-tuple-element.157), custom_call_target="InvertDiagBlocksLowerTriangular" | custom-call | tf_op jit(solution)/shard_map/jit(cholesky)/cholesky | solution.py:35
  472.0 12.9 %cholesky.415 = f32[128,128]{1,0:T(8,128)S(1)} custom-call(f32[128,128]{1,0:T(8,128)} %convolution_subtract_fusion.18), custom_call_target="Cholesky" | custom-call | tf_op jit(solution)/shard_map/jit(cholesky)/cholesky | solution.py:35
  491.6 40.1 %custom-call.35 = f32[4,128,128]{1,2,0:T(8,128)S(1)} custom-call(f32[4,128,128]{2,1,0:T(8,128)} %copy-done.11), custom_call_target="InvertDiagBlocksLowerTriangular" | custom-call | tf_op jit(solution)/shard_map/triangular_solve/custom-call.8 | solution.py:37
  532.5 80.8 %all-reduce.4.cloned.1.call-done = f32[512,147]{0,1:T(8,128)} async-done(((f32[512,147]{0,1:T(8,128)}), f32[512,147]{0,1:T(8,128)}) %all-reduce.4.cloned.1.call-update) | async-done | bytes 301072 | tf_op jit(solution)/shard_map/psum | solution.py:56
  621.8 1.4 convolution_subtract_fusion
  623.3 8.2 while.17
  624.1 1.3 bitcast_dynamic-update-slice_fusion.5
  626.1 1.3 bitcast_dynamic-update-slice_fusion.5
  628.2 1.3 bitcast_dynamic-update-slice_fusion.5
  630.2 1.3 bitcast_dynamic-update-slice_fusion.5
  631.5 39.3 %custom-call.40 = f32[4,128,128]{1,2,0:T(8,128)S(1)} custom-call(f32[4,128,128]{2,1,0:T(8,128)S(1)} %get-tuple-element.129), custom_call_target="InvertDiagBlocksLowerTriangular" | custom-call | tf_op jit(solution)/shard_map/triangular_solve/custom-call.8 | solution.py:37
  670.8 408.8 %all-reduce.6.cloned.1.call-done = f32[512,147]{0,1:T(8,128)} async-done(((f32[512,147]{0,1:T(8,128)}), f32[512,147]{0,1:T(8,128)}) %all-reduce.6.cloned.1.call-update) | async-done | bytes 301072 | tf_op jit(solution)/shard_map/psum | solution.py:56
  1086.7 1.7 scatter-add.9
  (152 shorter events, 54.9 us)
Async XLA Ops:
  6.5 5.0 copy-start.5
  6.5 606.7 %all-reduce.4.cloned.1.call-start = ((), (), s32[]{:S(2)}) async-start(), calls=%async_computation | async-start | bytes 622592 | tf_op jit(solution)/shard_map/psum | solution.py:56
  7.5 0.7 copy-start.14
  155.6 0.9 copy-start.12
  158.9 920.7 %all-reduce.6.cloned.1.call-start = ((), (), s32[]{:S(2)}) async-start(), calls=%async_computation.1 | async-start | bytes 622592 | tf_op jit(solution)/shard_map/psum | solution.py:56
  252.3 0.7 copy-start.11
  384.0 0.8 copy-start.3
  386.0 1.0 copy-start.1
  387.0 25.2 %copy-start.2 = (f32[512,512]{1,0:T(8,128)S(1)}, f32[512,512]{1,0:T(8,128)}, u32[]{:S(2)}) copy-start(f32[512,512]{1,0:T(8,128)} %copy-done.1) | copy-start | bytes 3145732
  398.7 0.6 copy-start.10
  413.7 0.7 copy-start.6
  442.7 0.7 copy-start.7
  490.2 1.0 copy-start.4
  491.6 40.1 %copy-start.15 = (s32[2]{0:T(128)S(1)}, s32[2]{0:T(128)}, u32[]{:S(2)}) copy-start(s32[2]{0:T(128)} %constant.173.clone.1) | copy-start | bytes 28
  614.5 1.6 copy-start.8
  620.3 0.9 copy-start.13
  621.2 464.6 %copy-start = (f32[256,147]{0,1:T(8,128)}, f32[256,147]{0,1:T(8,128)S(1)}, u32[]{:S(2)}) copy-start(f32[256,147]{0,1:T(8,128)S(1)} %scatter-add.6) | copy-start | bytes 451588
  1080.8 1.6 copy-start.9
Sparse Core Ops, SparseCore 0:
  159.0 454.2 all-reduce.3
  623.4 456.1 all-reduce.5
where the time goes:
time: 1100 us
  waiting for transfers between devices  490 us (45%)
  blocking collectives  272 us (25%)
  other arithmetic  254 us (23%)
  local copies, waits for them, and re-layouts  31.9 us (3%)
  matrix products  24 us (2%)
  between operations  23.3 us (2%)
    psum x2, waiting for transfers between devices, shards(): rhs = lax.psum(term, ('row', 'col'))  490 us
    all_gather x2, blocking collectives, shards(): lax.all_gather(frames[local_pick], ('row', 'col'), axis=0, tiled=True)  272 us
    another operation x30, other arithmetic, solve_block(): factor = jnp.linalg.cholesky(gram)  171 us
    another operation x5, other arithmetic, solve_block(): lax.linalg.triangular_solve(factor, middle, left_side=True, lower=True, t...  79.7 us
  transfers between devices with their start and end apart: 2, of which 2 were waited for; matrix products, arithmetic and copies ran while one was open for 26% of the time, Pallas kernels for 0%

commit v1 on v0

v1 whole, which is shorter than its diff:
```python
import functools

import jax
import jax.numpy as jnp
from jax import lax
from jax.experimental import pallas as pl
from jax.experimental.pallas import tpu as pltpu
from jax.sharding import Mesh, PartitionSpec as P

RIDGE = 1.0
LANES = 128
NEWTON_STEPS = 6
VMEM_BYTES = 48 * 1024 * 1024

NT = (((1,), (1,)), ((), ()))
NN = (((1,), (0,)), ((), ()))
TN = (((0,), (0,)), ((), ()))


def mm(a, b, dims=NN):
    return lax.dot_general(a, b, dims, preferred_element_type=jnp.float32)


def split(a):
    hi = a.astype(jnp.bfloat16)
    lo = (a - hi.astype(jnp.float32)).astype(jnp.bfloat16)
    return hi, lo


def mm3(a, b, dims=NN):
    return mm(a[0], b[0], dims) + (mm(a[0], b[1], dims) + mm(a[1], b[0], dims))


def mm6(a, b, dims=NN):
    return lax.dot_general(
        a, b, dims, precision=lax.Precision.HIGHEST, preferred_element_type=jnp.float32
    )


def eye_mask(n):
    return lax.broadcasted_iota(jnp.int32, (n, n), 0) == lax.broadcasted_iota(jnp.int32, (n, n), 1)


def inverses(mats):
    n = mats[0].shape[0]
    eye = jnp.where(eye_mask(n), 1.0, 0.0).astype(jnp.float32)
    state = []
    for a in mats:
        top = jnp.maximum(jnp.max(jnp.sum(jnp.abs(a), axis=1, keepdims=True), axis=0, keepdims=True), 1.5)
        scale = 2.0 / (1.0 + top)
        err = (top - 1.0) / (top + 1.0)
        gain = 2.0 / (2.0 - err * err)
        x = (gain * scale) * (2.0 * eye - scale * a)
        err = err * err * gain * 0.5
        state.append((a, split(a), x, err))
    for step in range(NEWTON_STEPS):
        later = []
        for a, parts, x, err in state:
            gain = 2.0 / (2.0 - err * err)
            if step < NEWTON_STEPS - 1:
                xs = split(x)
                y = mm3(parts, xs)
                x = gain * (2.0 * x - mm3(xs, split(y)))
            else:
                r = eye - mm6(a, x)
                x = gain * (x + mm3(split(x), split(r)))
            err = err * err * gain * 0.5
            later.append((a, parts, x, err))
        state = later
    return [s[2] for s in state]


def factor(grams):
    h = grams[0].shape[0] // 2
    firsts = inverses([g[:h, :h] for g in grams])
    couples = [mm6(x, g[:h, h:]) for x, g in zip(firsts, grams)]
    schurs = [g[h:, h:] - mm6(g[h:, :h], u) for g, u in zip(grams, couples)]
    seconds = inverses(schurs)
    return list(zip(firsts, couples, seconds, [g[h:, :h] for g in grams]))


def solve(parts, t):
    first, couple, second, lower = parts
    h = first.shape[0]
    y = mm6(first, t[:h])
    z = mm6(second, t[h:] - mm6(lower, y))
    return jnp.concatenate([y - mm6(couple, z), z], axis=0)


def pick_kernel(scal_ref, f0_ref, f1_ref, out_ref):
    feats = f0_ref.shape[1]
    rows = f0_ref.shape[0]
    for s, ref in enumerate((f0_ref, f1_ref)):
        at = scal_ref[s] % rows
        mask = lax.broadcasted_iota(jnp.int32, (rows, feats), 0) == at
        row = jnp.sum(jnp.where(mask, ref[...].astype(jnp.float32), 0.0), axis=0, keepdims=True)
        for c in range(4):
            lo = c * LANES
            wide = min(LANES, feats - lo)
            piece = row[:, lo : lo + wide]
            if wide < LANES:
                piece = jnp.concatenate([piece, jnp.zeros((1, LANES - wide), jnp.float32)], axis=1)
            out_ref[s * 4 + c : s * 4 + c + 1, :] = piece


def main_kernel(scal_ref, mine_ref, other_ref, frames_ref, sq_ref, weights_ref, labels_ref, same_ref, out_ref, wide_ref, lab_ref):
    rows, feats = frames_ref.shape
    targets = weights_ref.shape[1]
    half = mine_ref.shape[0]
    block = 2 * half
    factor_ = 0.5 / feats
    core = scal_ref[2]
    pos = scal_ref[3]
    mine = mine_ref[...]
    other = other_ref[...]
    flip = core == 0
    first = jnp.where(flip, mine, other)
    second = jnp.where(flip, other, mine)
    both = jnp.concatenate([first, second], axis=0)
    width = both.shape[1] // 2
    chosen = [both[:, :width], both[:, width:]]

    wide_ref[...] = jnp.zeros_like(wide_ref)
    wide_ref[:, :targets] = weights_ref[...]
    lab_ref[...] = jnp.zeros_like(lab_ref)
    lab_ref[:, :targets] = labels_ref[...].astype(jnp.float32)
    weights = wide_ref[...]
    frames = frames_ref[...]

    diag = eye_mask(block)
    inner = [mm(c, c, NT) for c in chosen]
    cross = mm(chosen[1], chosen[0], NT)
    tall = [jnp.sum(jnp.where(diag, g, 0.0), axis=1, keepdims=True) for g in inner]
    flat = [jnp.sum(jnp.where(diag, g, 0.0), axis=0, keepdims=True) for g in inner]
    one = jnp.where(diag, RIDGE, 0.0)
    grams = [jnp.exp(-(tall[s] + flat[s] - 2.0 * inner[s]) * factor_) + one for s in range(2)]
    between = jnp.exp(-(tall[1] + flat[0] - 2.0 * cross) * factor_)
    between = between + jnp.where(diag, RIDGE * same_ref[...], 0.0)

    here = lax.broadcasted_iota(jnp.int32, (block, 1), 0) == pos
    own = lab_ref[...] - RIDGE * weights
    at = lax.broadcasted_iota(jnp.int32, (rows, 1), 0)
    wsplit = split(weights)
    terms = []
    for s in range(2):
        near = jnp.exp(-(tall[s] + sq_ref[...] - 2.0 * mm(chosen[s][:, :feats], frames, NT)) * factor_)
        picked = jnp.sum(jnp.where(at == scal_ref[s], own, 0.0), axis=0, keepdims=True)
        terms.append(jnp.where(here, picked, 0.0) - mm3(split(near), wsplit))

    parts = factor(grams)
    delta0 = solve(parts[0], terms[0])
    delta1 = solve(parts[1], terms[1] - mm6(between, delta0))

    per = 16
    groups = half // per
    packed = None
    for s, d in enumerate((delta0, delta1)):
        body = d[:, :LANES].reshape(2, groups, per, LANES)
        rest = d[:, LANES:].reshape(2 * groups, 2, 8, LANES)
        for c in range(2):
            out_ref[:, c, s * per : (s + 1) * per, :] = body[c]
        for g in range(2):
            piece = rest[:, g].reshape(2 * groups * 8, LANES)
            turn = (2 * s + g) * 32
            if turn:
                piece = pltpu.roll(piece, turn, 1)
            packed = piece if packed is None else packed + piece
    packed = packed.reshape(2, groups, 8, LANES)
    for c in range(2):
        out_ref[:, c, 2 * per :, :] = packed[c]


def mid_kernel(got_ref, out_ref):
    total = jnp.sum(got_ref[...], axis=0)
    per = 16
    rest = total[2 * per :]
    for s in range(2):
        out_ref[:, s, :] = total[s * per : (s + 1) * per]
        halves = []
        for g in range(2):
            turn = (2 * s + g) * 32
            piece = pltpu.roll(rest, LANES - turn, 1) if turn else rest
            halves.append(piece)
        out_ref[:, 2 + s, :] = jnp.concatenate(halves, axis=0)


def end_kernel(scal_ref, got_ref, weights_ref, out_ref):
    rows, targets = weights_ref.shape
    total = jnp.sum(got_ref[...], axis=0)
    at = lax.broadcasted_iota(jnp.int32, (rows, 1), 0)
    out = weights_ref[...]
    for s in range(2):
        delta = jnp.concatenate([total[s : s + 1], total[2 + s : 3 + s]], axis=1)[:, :targets]
        out = out + jnp.where(at == scal_ref[s], delta, 0.0)
    out_ref[...] = out


def params():
    return pltpu.CompilerParams(vmem_limit_bytes=VMEM_BYTES)


VMEM = pl.BlockSpec(memory_space=pltpu.VMEM)
SMEM = pl.BlockSpec(memory_space=pltpu.SMEM)


def shards(frames, labels, weights, picks):
    rows, feats = frames.shape
    targets = weights.shape[1]
    n_xy, n_z, n_core = (lax.axis_size(a) for a in ("xy", "z", "core"))
    block = picks.shape[1]
    half = block // 2
    xy, z, core = (lax.axis_index(a) for a in ("xy", "z", "core"))
    device = (xy * n_z + z) * n_core + core
    pos = core * half + xy * n_z + z
    mine = lax.dynamic_slice(picks, (0, device), (2, 1)).reshape(2)
    scal = jnp.concatenate([mine, jnp.stack([core, pos]).astype(jnp.int32)])

    rowspec = lambda s: pl.BlockSpec((16, feats), lambda i, scal_ref: (scal_ref[s] // 16, 0))
    chosen = pl.pallas_call(
        pick_kernel,
        grid_spec=pltpu.PrefetchScalarGridSpec(
            num_scalar_prefetch=1,
            grid=(1,),
            in_specs=[rowspec(0), rowspec(1)],
            out_specs=pl.BlockSpec((8, LANES), lambda i, scal_ref: (0, 0)),
        ),
        out_shape=jax.ShapeDtypeStruct((8, LANES), jnp.float32),
    )(scal, frames, frames).astype(jnp.bfloat16)

    got = lax.all_to_all(jnp.broadcast_to(chosen[None], (n_z, 8, LANES)), "z", 0, 0)
    got = got.reshape(n_z, 8 * LANES)
    got = lax.all_to_all(jnp.broadcast_to(got[None], (n_xy,) + got.shape), "xy", 0, 0)
    got = got.reshape(half, 8 * LANES)
    other = lax.ppermute(got, "core", [(0, 1), (1, 0)])

    wide = frames.astype(jnp.float32)
    squares = jnp.sum(wide * wide, axis=1)[None, :]
    same = (picks[0] == picks[1]).astype(jnp.float32)
    same = same.reshape(n_xy * n_z, n_core).T.reshape(1, block)

    sent = pl.pallas_call(
        main_kernel,
        in_specs=[SMEM] + [VMEM] * 7,
        out_specs=VMEM,
        out_shape=jax.ShapeDtypeStruct((n_xy, n_core, 40, LANES), jnp.float32),
        scratch_shapes=[pltpu.VMEM((rows, 2 * LANES), jnp.float32)] * 2,
        compiler_params=params(),
    )(scal, got, other, frames, squares, weights, labels, same)

    got = lax.all_to_all(sent.reshape(n_xy * n_core, 40, LANES), ("xy", "core"), 0, 0)
    part = pl.pallas_call(
        mid_kernel,
        in_specs=[VMEM],
        out_specs=VMEM,
        out_shape=jax.ShapeDtypeStruct((n_z, 4, LANES), jnp.float32),
        compiler_params=params(),
    )(got)
    got = lax.all_to_all(part, "z", 0, 0)
    return pl.pallas_call(
        end_kernel,
        in_specs=[SMEM, VMEM, VMEM],
        out_specs=VMEM,
        out_shape=jax.ShapeDtypeStruct((rows, targets), jnp.float32),
        compiler_params=params(),
    )(scal, got, weights)


def solution(mesh):
    grid = Mesh(mesh.devices.reshape(mesh.shape["row"], -1, 2), ("xy", "z", "core"))
    spread = P(("xy", "z", "core"), None)
    return jax.shard_map(
        shards, mesh=grid, in_specs=(spread, spread, spread, P()), out_specs=spread, check_vma=False
    )
```

time: 1100 us -> 108 us (0.10)
  waiting for transfers between devices: 490 us -> 0.01 us
  other arithmetic: 254 us -> 1.41 us
  blocking collectives: 272 us -> 73.1 us
  local copies, waits for them, and re-layouts: 31.9 us -> 5.36 us
  matrix products: 24 us -> 0 us
  between operations: 23.3 us -> 0.1 us
  Pallas kernels: 0 us -> 22 us
    psum x2 -> x0, waiting for transfers between devices: 490 us -> none  [shards(): rhs = lax.psum(term, ('row', 'col'))]
    all_gather x2 -> x0, blocking collectives: 272 us -> none  [shards(): lax.all_gather(frames[local_pick], ('row', 'col'), axis=0, tiled=True)]
    another operation x38 -> x0, other arithmetic: 253 us -> none  [the longest x30 171 us: solve_block(): factor = jnp.linalg.cholesky(gram)]
    all_to_all x0 -> x4, blocking collectives: none -> 73.1 us  [the longest x1 27 us: shards(): lax.all_to_all(jnp.broadcast_to(chosen[None], (n_z, 8, LANES)), 'z', 0, 0)]
    pallas_call x0 -> x4, Pallas kernels: none -> 22 us  [the longest x1 19.3 us: shards(): pl.pallas_call(main_kernel, in_specs=[SMEM] + [VMEM] * 7, out_specs=VMEM,...]
    another operation x40 -> x0, matrix products: 19.2 us -> none  [the longest x14 7.93 us: solve_block(): lax.linalg.triangular_solve(factor, rhs, left_side=True, lower=True)]
    another operation x37 -> x0, local copies, waits for them, and re-layouts: 17.8 us -> none  [the longest x27 15.4 us: solve_block(): lax.linalg.triangular_solve(factor, middle, left_side=True, lower=True, t...]
  transfers between devices with their start and end apart: 2 -> 1, of which waited for: 2 -> 0; matrix products, arithmetic and copies ran while one was open for 26% -> 1% of each run, Pallas kernels for 0% -> 0%
where the time goes in v1:
time: 108 us; the launch traced here: 107 us
  blocking collectives  73.1 us (68%)
  Pallas kernels  22 us (20%)
  local copies, waits for them, and re-layouts  5.36 us (5%)
  starting transfers between devices  5.15 us (5%)
  other arithmetic  1.41 us (1%)
    all_to_all x1, blocking collectives, shards(): lax.all_to_all(jnp.broadcast_to(chosen[None], (n_z, 8, LANES)), 'z', 0, 0)  27 us
    pallas_call x1, Pallas kernels, shards(): pl.pallas_call(main_kernel, in_specs=[SMEM] + [VMEM] * 7, out_specs=VMEM,...  19.3 us
    all_to_all x1, blocking collectives, shards(): lax.all_to_all(sent.reshape(n_xy * n_core, 40, LANES), ('xy', 'core'), 0, 0)  16.3 us
    all_to_all x1, blocking collectives, shards(): lax.all_to_all(jnp.broadcast_to(got[None], (n_xy,) + got.shape), 'xy', 0, 0)  15.8 us
    all_to_all x1, blocking collectives, shards(): got = lax.all_to_all(part, 'z', 0, 0)  14 us
    ppermute x1, starting transfers between devices, shards(): other = lax.ppermute(got, 'core', [(0, 1), (1, 0)])  5.15 us
    unnamed x17, local copies, waits for them, and re-layouts  4.14 us
  transfers between devices with their start and end apart: 1, of which 0 were waited for; matrix products, arithmetic and copies ran while one was open for 1% of the time, Pallas kernels for 0%

profile of v1, /device:TPU:1, one launch (start us, length us, event | category | flops | bytes accessed | tf_op | source)
XLA Modules:
  0.0 107.2 jit_solution(13344313877701125522)
XLA Ops:
  0.0 0.0 copy-start.5
  0.0 1.8 %copy.13.f0_ref.f1_ref.frames_ref = bf16[256,440]{1,0:T(8,128)(2,1)} copy(bf16[256,440]{0,1:T(8,128)(2,1)} %param.4) | data formatting | bytes 450560 | tf_op args[0]
  1.8 0.0 copy-done.5
  1.8 0.2 dynamic-slice_reduce_fusion
  2.0 0.6 pad_add_fusion.scal_ref
  2.6 2.0 %shard_map.46 = f32[8,128]{1,0:T(8,128)} custom-call(s32[4]{0:T(128)} %pad_add_fusion.scal_ref, bf16[256,440]{1,0:T(8,128)(2,1)} %copy.13.f0_ref.f1_ref.frames_ref, bf16[256,440]{1,0:T(8,128)(2,1)} %copy.13.f0_ref.f1_ref.frames_ref), custom_call_target="tpu_custom_call" | custom-call | tf_op jit(solution)/shard_map/pallas_call | solution.py:219
  4.6 0.7 convert_element_type.11
  5.3 27.0 %all_to_all.20 = bf16[16,8,128]{2,1,0:T(8,128)(2,1)S(1)} all-to-all(bf16[16,8,128]{2,1,0:T(8,128)(2,1)S(1)} %broadcast_in_dim.16), channel_id=1, replica_groups=mesh['xy'=16,'z'=16,'core'=2] {'z'}, dimensions={0} | all-to-all | bytes 65536 | tf_op jit(solution)/shard_map/all_to_all | solution.py:230
  32.3 0.1 broadcast_in_dim.18
  32.4 15.8 %all_to_all.21 = bf16[16,16,1024]{2,1,0:T(8,128)(2,1)S(1)} all-to-all(bf16[16,16,1024]{2,1,0:T(8,128)(2,1)S(1)} %broadcast_in_dim.18), channel_id=1, replica_groups=mesh['xy'=16,'z'=16,'core'=2] {'xy'}, dimensions={0} | all-to-all | bytes 1048576 | tf_op jit(solution)/shard_map/all_to_all | solution.py:232
  48.1 5.1 %collective-permute-start = (bf16[256,1024]{1,0:T(8,128)(2,1)S(1)}, bf16[256,1024]{1,0:T(8,128)(2,1)S(1)}, u32[]{:S(2)}, u32[]{:S(2)}) collective-permute-start(bf16[256,1024]{1,0:T(8,128)(2,1)S(1)} %bitcast.14), channel_id=1, source_target_pairs={{0,1},{1,0},{2,3},{3,2},{4,5},{5,4},{6,7},{7,6},{8,9},{9,8},{10,11... | collective-permute-start | bytes 1572872 | tf_op jit(solution)/shard_map/ppermute | solution.py:234
  53.3 0.1 reshape.31
  53.5 0.0 copy-start.4
  53.5 0.0 copy-start.3
  53.5 0.1 copy.15
  53.6 0.8 copy-done.4
  54.3 0.0 copy-start.2
  54.3 0.1 copy.18.labels_ref
  54.4 0.0 copy-done.3
  54.5 0.0 copy-start
  54.5 0.1 copy.17.weights_ref
  54.6 0.7 copy-done.2
  55.3 0.1 multiply_reduce_fusion
  55.4 0.0 collective-permute-done.other_ref
  55.4 0.0 copy-done
  55.4 0.6 copy-done.1
  56.0 19.3 %shard_map.47 = f32[16,2,40,128]{3,2,1,0:T(8,128)S(1)} custom-call(s32[4]{0:T(128)S(1)} %copy-done.1, bf16[256,1024]{1,0:T(8,128)(2,1)S(1)} %bitcast.15, bf16[256,1024]{1,0:T(8,128)(2,1)S(1)} %collective-permute-done.other_ref, bf16[256,440]{1,0:T(8,128)(2,1)S(1)} %copy-done, f32[1,256]{1,0:T(1,128)S(1)} %bitcast.17, f32[256,147]{1,0:T(8,128)S(1)} %copy.17.weights_ref, ...), custom_call_target="tpu_custom_call" | custom-call | tf_op jit(solution)/shard_map/pallas_call | solution.py:241
  75.3 16.3 %all_to_all.22.got_ref = f32[32,40,128]{2,1,0:T(8,128)S(1)} all-to-all(f32[32,40,128]{2,1,0:T(8,128)S(1)} %bitcast.13), channel_id=1, replica_groups=mesh['xy'=16,'z'=16,'core'=2] {'xy','core'}, dimensions={0} | all-to-all | bytes 1310720 | tf_op jit(solution)/shard_map/all_to_all | solution.py:250
  91.7 0.1 shard_map.48
  91.8 14.0 %all_to_all.23.got_ref = f32[16,4,128]{2,1,0:T(4,128)S(1)} all-to-all(f32[16,4,128]{2,1,0:T(4,128)S(1)} %shard_map.48), channel_id=1, replica_groups=mesh['xy'=16,'z'=16,'core'=2] {'z'}, dimensions={0} | all-to-all | bytes 65536 | tf_op jit(solution)/shard_map/all_to_all | solution.py:258
  105.8 0.6 shard_map.49
  106.4 0.8 copy.20
  (5 shorter events, 0.0 us)
Async XLA Ops:
  0.0 1.8 %copy-start.5 = (s32[2,512]{1,0:T(2,128)S(1)}, s32[2,512]{1,0:T(2,128)}, u32[]{:S(2)}) copy-start(s32[2,512]{1,0:T(2,128)} %param.7) | copy-start | bytes 12292
  48.1 7.3 %collective-permute-start = (bf16[256,1024]{1,0:T(8,128)(2,1)S(1)}, bf16[256,1024]{1,0:T(8,128)(2,1)S(1)}, u32[]{:S(2)}, u32[]{:S(2)}) collective-permute-start(bf16[256,1024]{1,0:T(8,128)(2,1)S(1)} %bitcast.14), channel_id=1, source_target_pairs={{0,1},{1,0},{2,3},{3,2},{4,5},{5,4},{6,7},{7,6},{8,9},{9,8},{10,11... | collective-permute-start | bytes 1572872 | tf_op jit(solution)/shard_map/ppermute | solution.py:234
  53.5 0.9 copy-start.4
  53.5 1.0 copy-start.3
  54.3 1.0 copy-start.2
  54.5 1.0 copy-start
  55.4 0.6 copy-start.1

commit v2 on v0

v2 whole, which is shorter than its diff:
```python
import jax
import jax.numpy as jnp
from jax import lax
from jax.experimental import pallas as pl
from jax.experimental.pallas import tpu as pltpu
from jax.sharding import Mesh, PartitionSpec as P

RIDGE = 1.0
LANES = 128
JOINT_STEPS = 3
VMEM_BYTES = 40 * 1024 * 1024

NN = (((1,), (0,)), ((), ()))
NT = (((1,), (1,)), ((), ()))


def mm(a, b, dims=NN):
    return lax.dot_general(a, b, dims, preferred_element_type=jnp.float32)


def mm6(a, b, dims=NN):
    return lax.dot_general(
        a, b, dims, precision=lax.Precision.HIGHEST, preferred_element_type=jnp.float32
    )


def split(a):
    hi = a.astype(jnp.bfloat16)
    lo = (a - hi.astype(jnp.float32)).astype(jnp.bfloat16)
    return hi, lo


def mm3(a, b, dims=NN):
    rows = a[0].shape[0]
    left = mm(jnp.concatenate(a, axis=0), b[0], dims)
    return left[:rows] + (left[rows:] + mm(a[0], b[1], dims))


def eye_mask(n):
    return lax.broadcasted_iota(jnp.int32, (n, n), 0) == lax.broadcasted_iota(jnp.int32, (n, n), 1)


def inverses(mats):
    n = mats[0].shape[0]
    eye = jnp.where(eye_mask(n), 1.0, 0.0).astype(jnp.float32)
    state = []
    for a in mats:
        top = jnp.max(jnp.sum(jnp.abs(a), axis=0, keepdims=True), axis=1, keepdims=True)
        top = jnp.maximum(top, 1.5)
        scale = 2.0 / (1.0 + top)
        err = (top - 1.0) / (top + 1.0)
        gain = 2.0 / (2.0 - err * err)
        r = eye - scale * a
        x = (gain * scale) * (eye + r)
        rs = split(r)
        r = (1.0 - gain) * eye + gain * mm3(rs, rs)
        state.append((x, r, err * err * gain * 0.5))
    for step in range(JOINT_STEPS + 1):
        later = []
        for x, r, err in state:
            gain = 2.0 / (2.0 - err * err)
            rs = split(r)
            xs = split(x)
            if step < JOINT_STEPS:
                left = mm(jnp.concatenate(xs + rs, axis=0), rs[0])
                square = left[2 * n : 3 * n] + (left[3 * n :] + mm(rs[0], rs[1]))
                r = (1.0 - gain) * eye + gain * square
            else:
                left = mm(jnp.concatenate(xs, axis=0), rs[0])
            x = gain * (x + (left[:n] + left[n : 2 * n]))
            later.append((x, r, err * err * gain * 0.5))
        state = later
    for last in (False, True):
        later = []
        for a, (x, r, err) in zip(mats, state):
            gain = 2.0 / (2.0 - err * err)
            xs = split(x)
            r = eye - (mm6(a, x) if last else mm3(split(a), xs))
            left = mm(jnp.concatenate(xs, axis=0), r.astype(jnp.bfloat16))
            x = gain * (x + (left[:n] + left[n:]))
            later.append((x, r, err * err * gain * 0.5))
        state = later
    return [s[0] for s in state]


def place():
    xy, z, core = (lax.axis_index(a) for a in ("xy", "z", "core"))
    n_z, n_core = lax.axis_size("z"), lax.axis_size("core")
    return (xy * n_z + z) * n_core + core, xy * n_z + z, core


def onehots(picks_ref, device, rows):
    at = lax.broadcasted_iota(jnp.int32, (8, rows), 1)
    row = lax.broadcasted_iota(jnp.int32, (8, rows), 0)
    want = jnp.where(row == 0, picks_ref[0, device], jnp.where(row == 1, picks_ref[1, device], -1))
    return jnp.where(at == want, 1.0, 0.0)


def pick_kernel(picks_ref, frames_ref, out_ref):
    feats, rows = frames_ref.shape
    device, _, _ = place()
    chosen = mm(onehots(picks_ref, device, rows).astype(jnp.bfloat16), frames_ref[...], NT)
    same = jnp.where(picks_ref[0, device] == picks_ref[1, device], 1.0, 0.0)
    lane = lax.broadcasted_iota(jnp.int32, (1, LANES), 1)
    parts = []
    for s in range(2):
        for c in range(4):
            lo = c * LANES
            wide = min(LANES, feats - lo)
            piece = chosen[s : s + 1, lo : lo + wide]
            if wide < LANES:
                piece = jnp.concatenate([piece, jnp.zeros((1, LANES - wide), jnp.float32)], axis=1)
                piece = jnp.where(lane == wide, same, piece)
            parts.append(piece)
    row = jnp.concatenate(parts, axis=0).astype(jnp.bfloat16)
    out_ref[...] = jnp.broadcast_to(row[None], out_ref.shape)


def halves(ref, feats):
    width = ref.shape[1] // 2
    return [ref[:, s * width : s * width + feats] for s in range(2)]


def gauss(tall, flat, inner, feats):
    return jnp.exp(-(tall + flat - 2.0 * inner) * (0.5 / feats))


def diag_sums(inner, diag):
    masked = jnp.where(diag, inner, 0.0)
    return jnp.sum(masked, axis=1, keepdims=True), jnp.sum(masked, axis=0, keepdims=True)


def term_of(chosen, tall, frames, frame_sq, wsplit, feats):
    near = gauss(tall, frame_sq, mm(chosen, frames), feats)
    return mm3(wsplit, split(near), NT)


def frame_squares(frames):
    wide = frames.astype(jnp.float32)
    return jnp.sum(wide * wide, axis=0, keepdims=True)


def padded(ref, scratch):
    scratch[...] = jnp.zeros_like(scratch)
    scratch[: ref.shape[0], :] = ref[...].astype(jnp.float32)
    return scratch[...]


def own_kernel(picks_ref, own_ref, frames_ref, weights_ref, labels_ref, inv_ref, term_ref, tall_ref, flat_ref, w_scr, l_scr):
    feats, rows = frames_ref.shape
    half = own_ref.shape[0]
    device, pos, _ = place()
    chosen = halves(own_ref, feats)
    diag = eye_mask(half)
    one = jnp.where(diag, RIDGE, 0.0)
    inner = [mm(c, c, NT) for c in chosen]
    sums = [diag_sums(g, diag) for g in inner]
    mats = [gauss(t, f, g, feats) + one for (t, f), g in zip(sums, inner)]
    inv = inverses(mats)
    for s in range(2):
        inv_ref[s] = inv[s]
        flat_ref[s : s + 1, :] = sums[s][1]
        tall_ref[:, s : s + 1] = sums[s][0]
    frames = frames_ref[...]
    frame_sq = frame_squares(frames)
    weights = padded(weights_ref, w_scr)
    wsplit = split(weights)
    start = padded(labels_ref, l_scr) - RIDGE * weights
    hot = onehots(picks_ref, device, rows)
    here = lax.broadcasted_iota(jnp.int32, (1, half), 1) == pos
    for s in range(2):
        picked = jnp.sum(start * hot[s : s + 1], axis=1, keepdims=True)
        term = term_of(chosen[s], sums[s][0], frames, frame_sq, wsplit, feats)
        term_ref[s] = jnp.where(here, picked, 0.0) - term


def rest_kernel(own_ref, other_ref, frames_ref, weights_ref, inv_ref, term_ref, tall_ref, flat_ref, out_ref, w_scr):
    feats, rows = frames_ref.shape
    half = own_ref.shape[0]
    _, _, core = place()
    near = halves(own_ref, feats)
    far = halves(other_ref, feats)
    diag = eye_mask(half)
    one = jnp.where(diag, RIDGE, 0.0)
    inner = [mm(c, c, NT) for c in far]
    sums = [diag_sums(g, diag) for g in inner]
    talls = [[tall_ref[:, s : s + 1], sums[s][0]] for s in range(2)]
    flats = [[flat_ref[s : s + 1, :], sums[s][1]] for s in range(2)]
    chosen = [[near[s], far[s]] for s in range(2)]

    def block(s, i, t, j):
        return gauss(talls[s][i], flats[t][j], mm(chosen[s][i], chosen[t][j], NT), feats)

    inv, couple, lower, upper, schur = [], [], [], [], []
    for s in range(2):
        inv.append(inv_ref[s])
        upper.append(block(s, 0, s, 1))
        lower.append(block(s, 1, s, 0))
        couple.append(mm6(inv[s], upper[s]))
        corner = gauss(talls[s][1], flats[s][1], inner[s], feats) + one
        schur.append(corner - mm6(lower[s], couple[s]))
    inv2 = inverses(schur)

    frames = frames_ref[...]
    frame_sq = frame_squares(frames)
    wsplit = split(padded(weights_ref, w_scr))
    width = own_ref.shape[1] // 2
    flags = [r[:, width + feats : width + feats + 1].astype(jnp.float32) for r in (own_ref, other_ref)]
    deltas = []
    for s in range(2):
        first = term_ref[s]
        second = -term_of(far[s], talls[s][1], frames, frame_sq, wsplit, feats)
        if s == 1:
            cross = [[block(1, i, 0, j) for j in range(2)] for i in range(2)]
            for i in range(2):
                cross[i][i] = cross[i][i] + jnp.where(diag, RIDGE * flags[i], 0.0)
            first = first - (mm6(deltas[0][0], cross[0][0], NT) + mm6(deltas[0][1], cross[0][1], NT))
            second = second - (mm6(deltas[0][0], cross[1][0], NT) + mm6(deltas[0][1], cross[1][1], NT))
        y = mm6(first, inv[s])
        z = mm6(second - mm6(y, upper[s]), inv2[s])
        deltas.append((y - mm6(z, couple[s], NT), z))

    per = 16
    groups = half // per
    fill = jnp.zeros((2 * LANES - deltas[0][0].shape[0], half), jnp.float32)
    for i, slot in enumerate((core, 1 - core)):
        packed = None
        for s in range(2):
            full = jnp.concatenate([deltas[s][i], fill], axis=0)
            body = jnp.transpose(full[:LANES])
            out_ref[:, pl.ds(slot, 1), s * per : (s + 1) * per, :] = body.reshape(groups, 1, per, LANES)
            tail = jnp.transpose(full[LANES:]).reshape(groups, 2, 8, LANES)
            for g in range(2):
                piece = tail[:, g].reshape(groups * 8, LANES)
                turn = (2 * s + g) * 32
                if turn:
                    piece = pltpu.roll(piece, turn, 1)
                packed = piece if packed is None else packed + piece
        out_ref[:, pl.ds(slot, 1), 2 * per :, :] = packed.reshape(groups, 1, 8, LANES)


def mid_kernel(got_ref, out_ref):
    total = jnp.sum(got_ref[...], axis=0)
    per = 16
    rest = total[2 * per :]
    for s in range(2):
        out_ref[:, s, :] = total[s * per : (s + 1) * per]
        pieces = []
        for g in range(2):
            turn = (2 * s + g) * 32
            pieces.append(pltpu.roll(rest, LANES - turn, 1) if turn else rest)
        out_ref[:, 2 + s, :] = jnp.concatenate(pieces, axis=0)


def end_kernel(picks_ref, got_ref, weights_ref, out_ref):
    targets, rows = weights_ref.shape
    device, _, _ = place()
    total = jnp.sum(got_ref[...], axis=0)
    turned = jnp.transpose(jnp.concatenate([total, jnp.zeros((LANES - 4, LANES), jnp.float32)], axis=0))
    hot = onehots(picks_ref, device, rows)
    out_ref[:LANES, :] = weights_ref[:LANES, :] + (turned[:, 0:1] * hot[0:1] + turned[:, 1:2] * hot[1:2])
    left = targets - LANES
    out_ref[LANES:, :] = weights_ref[LANES:, :] + (
        turned[:left, 2:3] * hot[0:1] + turned[:left, 3:4] * hot[1:2]
    )


VMEM = pl.BlockSpec(memory_space=pltpu.VMEM)
SMEM = pl.BlockSpec(memory_space=pltpu.SMEM)


def kernel(body, ins, outs, scratch=(), flops=0):
    single = not isinstance(outs, list)
    return pl.pallas_call(
        body,
        in_specs=ins,
        out_specs=VMEM if single else [VMEM] * len(outs),
        out_shape=outs,
        scratch_shapes=list(scratch),
        compiler_params=pltpu.CompilerParams(vmem_limit_bytes=VMEM_BYTES),
        cost_estimate=pl.CostEstimate(flops=flops, bytes_accessed=1 << 20, transcendentals=0),
    )


def f32(*dims):
    return jax.ShapeDtypeStruct(dims, jnp.float32)


def update(got, other, frames, weights, labels, picks, n_xy):
    half = got.shape[0]
    targets, rows = weights.shape
    tall = -(-targets // 8) * 8
    scratch = pltpu.VMEM((tall, rows), jnp.float32)
    known = kernel(
        own_kernel,
        [SMEM] + [VMEM] * 4,
        [f32(2, half, half), f32(2, tall, half), f32(half, 2), f32(2, half)],
        [scratch, scratch],
        flops=6_000_000_000,
    )(picks, got, frames, weights, labels)
    return kernel(rest_kernel, [VMEM] * 8, f32(n_xy, 2, 40, LANES), [scratch], flops=6_000_000_000)(
        got, other, frames, weights, *known
    )


def shards(frames, labels, weights, picks):
    n_xy, n_z, n_core = (lax.axis_size(a) for a in ("xy", "z", "core"))
    frames, labels, weights = frames.T, labels.T, weights.T
    sent = kernel(pick_kernel, [SMEM, VMEM], jax.ShapeDtypeStruct((n_z, 8, LANES), jnp.bfloat16))(picks, frames)
    got = lax.all_to_all(sent, "z", 0, 0).reshape(n_z, 8 * LANES)
    got = lax.all_to_all(jnp.broadcast_to(got[None], (n_xy,) + got.shape), "xy", 0, 0)
    got = got.reshape(n_xy * n_z, 8 * LANES)
    other = lax.ppermute(got, "core", [(0, 1), (1, 0)])
    sent = update(got, other, frames, weights, labels, picks, n_xy)
    got = lax.all_to_all(sent.reshape(n_xy * n_core, 40, LANES), ("xy", "core"), 0, 0)
    part = kernel(mid_kernel, [VMEM], f32(n_z, 4, LANES))(got)
    got = lax.all_to_all(part, "z", 0, 0)
    return kernel(end_kernel, [SMEM, VMEM, VMEM], f32(*weights.shape))(picks, got, weights).T


def solution(mesh):
    grid = Mesh(mesh.devices.reshape(mesh.shape["row"], -1, 2), ("xy", "z", "core"))
    spread = P(("xy", "z", "core"), None)
    return jax.shard_map(
        shards, mesh=grid, in_specs=(spread, spread, spread, P()), out_specs=spread, check_vma=False
    )
```

time: 1100 us -> 101 us (0.09)
  waiting for transfers between devices: 490 us -> 0.01 us
  other arithmetic: 254 us -> 0 us
  blocking collectives: 272 us -> 73.3 us
  local copies, waits for them, and re-layouts: 31.9 us -> 1.7 us
  matrix products: 24 us -> 0 us
  between operations: 23.3 us -> 0.09 us
  Pallas kernels: 0 us -> 20.2 us
    psum x2 -> x0, waiting for transfers between devices: 490 us -> none  [shards(): rhs = lax.psum(term, ('row', 'col'))]
    all_gather x2 -> x0, blocking collectives: 272 us -> none  [shards(): lax.all_gather(frames[local_pick], ('row', 'col'), axis=0, tiled=True)]
    another operation x38 -> x0, other arithmetic: 253 us -> none  [the longest x30 171 us: solve_block(): factor = jnp.linalg.cholesky(gram)]
    all_to_all x0 -> x4, blocking collectives: none -> 73.3 us  [the longest x1 27 us: shards(): got = lax.all_to_all(sent, 'z', 0, 0).reshape(n_z, 8 * LANES)]
    pallas_call x0 -> x5, Pallas kernels: none -> 20.2 us  [the longest x1 11.5 us: update(): kernel(rest_kernel, [VMEM] * 8, f32(n_xy, 2, 40, LANES), [scratch], flops...]
    another operation x40 -> x0, matrix products: 19.2 us -> none  [the longest x14 7.93 us: solve_block(): lax.linalg.triangular_solve(factor, rhs, left_side=True, lower=True)]
    another operation x37 -> x0, local copies, waits for them, and re-layouts: 17.8 us -> none  [the longest x27 15.4 us: solve_block(): lax.linalg.triangular_solve(factor, middle, left_side=True, lower=True, t...]
  transfers between devices with their start and end apart: 2 -> 1, of which waited for: 2 -> 0; matrix products, arithmetic and copies ran while one was open for 26% -> 0% of each run, Pallas kernels for 0% -> 6%
where the time goes in v2:
time: 101 us; the launch traced here: 100 us
  blocking collectives  73.3 us (73%)
  Pallas kernels  20.2 us (20%)
  starting transfers between devices  5.15 us (5%)
  local copies, waits for them, and re-layouts  1.7 us (2%)
    all_to_all x1, blocking collectives, shards(): got = lax.all_to_all(sent, 'z', 0, 0).reshape(n_z, 8 * LANES)  27 us
    all_to_all x1, blocking collectives, shards(): lax.all_to_all(sent.reshape(n_xy * n_core, 40, LANES), ('xy', 'core'), 0, 0)  16.3 us
    all_to_all x1, blocking collectives, shards(): lax.all_to_all(jnp.broadcast_to(got[None], (n_xy,) + got.shape), 'xy', 0, 0)  15.9 us
    all_to_all x1, blocking collectives, shards(): got = lax.all_to_all(part, 'z', 0, 0)  14 us
    pallas_call x1, Pallas kernels, update(): kernel(rest_kernel, [VMEM] * 8, f32(n_xy, 2, 40, LANES), [scratch], flops...  11.5 us
    pallas_call x1, Pallas kernels, update(): kernel(own_kernel, [SMEM] + [VMEM] * 4, [f32(2, half, half), f32(2, tall,...  6.33 us
    ppermute x1, starting transfers between devices, shards(): other = lax.ppermute(got, 'core', [(0, 1), (1, 0)])  5.15 us
  transfers between devices with their start and end apart: 1, of which 0 were waited for; matrix products, arithmetic and copies ran while one was open for 0% of the time, Pallas kernels for 6%

profile of v2, /device:TPU:1, one launch (start us, length us, event | category | flops | bytes accessed | tf_op | source)
XLA Modules:
  0.0 100.4 jit_solution(198371316430245037)
XLA Ops:
  0.0 0.0 copy-start
  0.0 0.9 copy-done
  0.9 0.0 copy-start.2
  0.9 0.7 copy-done.2
  1.6 0.8 shard_map.46
  2.4 27.0 %all_to_all.20 = bf16[16,8,128]{2,1,0:T(8,128)(2,1)S(1)} all-to-all(bf16[16,8,128]{2,1,0:T(8,128)(2,1)S(1)} %shard_map.46), channel_id=1, replica_groups=mesh['xy'=16,'z'=16,'core'=2] {'z'}, dimensions={0} | all-to-all | bytes 65536 | tf_op jit(solution)/shard_map/all_to_all | solution.py:310
  29.4 0.1 broadcast_in_dim.8
  29.5 0.0 copy-start.1
  29.5 0.0 copy-start.4
  29.5 15.9 %all_to_all.21 = bf16[16,16,1024]{2,1,0:T(8,128)(2,1)S(1)} all-to-all(bf16[16,16,1024]{2,1,0:T(8,128)(2,1)S(1)} %broadcast_in_dim.8), channel_id=1, replica_groups=mesh['xy'=16,'z'=16,'core'=2] {'xy'}, dimensions={0} | all-to-all | bytes 1048576 | tf_op jit(solution)/shard_map/all_to_all | solution.py:311
  45.4 5.1 %collective-permute-start = (bf16[256,1024]{1,0:T(8,128)(2,1)S(1)}, bf16[256,1024]{1,0:T(8,128)(2,1)S(1)}, u32[]{:S(2)}, u32[]{:S(2)}) collective-permute-start(bf16[256,1024]{1,0:T(8,128)(2,1)S(1)} %bitcast.11), channel_id=1, source_target_pairs={{0,1},{1,0},{2,3},{3,2},{4,5},{5,4},{6,7},{7,6},{8,9},{9,8},{10,11... | collective-permute-start | bytes 1572872 | tf_op jit(solution)/shard_map/ppermute | solution.py:313
  50.6 0.0 copy-done.1
  50.6 0.0 copy-done.4
  50.6 6.3 %shard_map.47 = (f32[2,256,256]{2,1,0:T(8,128)S(1)}, f32[2,152,256]{2,1,0:T(8,128)S(1)}, f32[256,2]{1,0:T(8,128)S(1)}, f32[2,256]{1,0:T(2,128)S(1)}) custom-call(s32[2,512]{1,0:T(2,128)S(1)} %copy-done.2, bf16[256,1024]{1,0:T(8,128)(2,1)S(1)} %bitcast.12, bf16[440,256]{1,0:T(8,128)(2,1)S(1)} %bitcast.15, f32[147,256]{1,0:T(8,128)S(1)} %bitcast.17, ...), custom_call_target="tpu_custom_call" | custom-call | flops 6000000000 | bytes 1048576 | tf_op jit(solution)/shard_map/pallas_call | solution.py:294
  56.9 0.0 collective-permute-done.other_ref
  56.9 11.5 %shard_map.48 = f32[16,2,40,128]{3,2,1,0:T(8,128)S(1)} custom-call(bf16[256,1024]{1,0:T(8,128)(2,1)S(1)} %bitcast.13, bf16[256,1024]{1,0:T(8,128)(2,1)S(1)} %collective-permute-done.other_ref, bf16[440,256]{1,0:T(8,128)(2,1)S(1)} %bitcast.16, f32[147,256]{1,0:T(8,128)S(1)} %bitcast.18, f32[2,256,256]{2,1,0:T(8,128)S(1)} %get-tuple-element.9.inv_ref, ...), custom_call_target="tpu_custom_call" | custom-call | flops 6000000000 | bytes 1048576 | tf_op jit(solution)/shard_map/pallas_call | solution.py:301
  68.4 16.3 %all_to_all.22.got_ref = f32[32,40,128]{2,1,0:T(8,128)S(1)} all-to-all(f32[32,40,128]{2,1,0:T(8,128)S(1)} %bitcast.10), channel_id=1, replica_groups=mesh['xy'=16,'z'=16,'core'=2] {'xy','core'}, dimensions={0} | all-to-all | bytes 1310720 | tf_op jit(solution)/shard_map/all_to_all | solution.py:315
  84.8 0.1 shard_map.49
  84.9 0.0 copy-start.3
  84.9 14.0 %all_to_all.23.got_ref = f32[16,4,128]{2,1,0:T(4,128)S(1)} all-to-all(f32[16,4,128]{2,1,0:T(4,128)S(1)} %shard_map.49), channel_id=1, replica_groups=mesh['xy'=16,'z'=16,'core'=2] {'z'}, dimensions={0} | all-to-all | bytes 65536 | tf_op jit(solution)/shard_map/all_to_all | solution.py:317
  98.9 0.0 copy-done.3
  98.9 1.5 %shard_map.50 = f32[147,256]{1,0:T(8,128)} custom-call(s32[2,512]{1,0:T(2,128)S(1)} %copy-done.3, f32[16,4,128]{2,1,0:T(4,128)S(1)} %all_to_all.23.got_ref, f32[147,256]{1,0:T(8,128)S(1)} %bitcast.19), custom_call_target="tpu_custom_call" | custom-call | bytes 1048576 | tf_op jit(solution)/shard_map/pallas_call | solution.py:318
  (1 shorter events, 0.0 us)
Async XLA Ops:
  0.0 0.9 copy-start
  0.9 0.7 copy-start.2
  29.5 21.1 %copy-start.1 = (f32[256,147]{0,1:T(8,128)S(1)}, f32[256,147]{0,1:T(8,128)}, u32[]{:S(2)}) copy-start(f32[256,147]{0,1:T(8,128)} %param.6) | copy-start | bytes 451588
  29.5 21.1 %copy-start.4 = (bf16[256,147]{0,1:T(8,128)(2,1)S(1)}, bf16[256,147]{0,1:T(8,128)(2,1)}, u32[]{:S(2)}) copy-start(bf16[256,147]{0,1:T(8,128)(2,1)} %param.5) | copy-start | bytes 225796
  45.4 11.5 %collective-permute-start = (bf16[256,1024]{1,0:T(8,128)(2,1)S(1)}, bf16[256,1024]{1,0:T(8,128)(2,1)S(1)}, u32[]{:S(2)}, u32[]{:S(2)}) collective-permute-start(bf16[256,1024]{1,0:T(8,128)(2,1)S(1)} %bitcast.11), channel_id=1, source_target_pairs={{0,1},{1,0},{2,3},{3,2},{4,5},{5,4},{6,7},{7,6},{8,9},{9,8},{10,11... | collective-permute-start | bytes 1572872 | tf_op jit(solution)/shard_map/ppermute | solution.py:313
  84.9 14.0 %copy-start.3 = (s32[2,512]{1,0:T(2,128)S(1)}, s32[2,512]{1,0:T(2,128)}, u32[]{:S(2)}) copy-start(s32[2,512]{1,0:T(2,128)} %picks_ref.5) | copy-start | bytes 12292

commit v3 on v2

--- a/solution.py
+++ b/solution.py
@@ -7,7 +7,7 @@
 
 RIDGE = 1.0
 LANES = 128
-JOINT_STEPS = 3
+JOINT_STEPS = 4
 VMEM_BYTES = 40 * 1024 * 1024
 
 NN = (((1,), (0,)), ((), ()))
@@ -16,12 +16,6 @@
 
 def mm(a, b, dims=NN):
     return lax.dot_general(a, b, dims, preferred_element_type=jnp.float32)
-
-
-def mm6(a, b, dims=NN):
-    return lax.dot_general(
-        a, b, dims, precision=lax.Precision.HIGHEST, preferred_element_type=jnp.float32
-    )
 
 
 def split(a):
@@ -30,17 +24,66 @@
     return hi, lo
 
 
+def split3(a):
+    hi = a.astype(jnp.bfloat16)
+    rest = a - hi.astype(jnp.float32)
+    mid = rest.astype(jnp.bfloat16)
+    return hi, mid, (rest - mid.astype(jnp.float32)).astype(jnp.bfloat16)
+
+
+def joined(left, right, dims):
+    return mm(jnp.concatenate(left, axis=dims[0][0][0]), jnp.concatenate(right, axis=dims[0][1][0]), dims)
+
+
 def mm3(a, b, dims=NN):
-    rows = a[0].shape[0]
-    left = mm(jnp.concatenate(a, axis=0), b[0], dims)
-    return left[:rows] + (left[rows:] + mm(a[0], b[1], dims))
+    return joined((a[0], a[1], a[0]), (b[0], b[0], b[1]), dims)
+
+
+def split(a):
+    hi = a.astype(jnp.bfloat16)
+    lo = (a - hi.astype(jnp.float32)).astype(jnp.bfloat16)
+    return hi, lo
+
+
+def split3(a):
+    hi = a.astype(jnp.bfloat16)
+    rest = a - hi.astype(jnp.float32)
+    mid = rest.astype(jnp.bfloat16)
+    return hi, mid, (rest - mid.astype(jnp.float32)).astype(jnp.bfloat16)
+
+
+def joined(left, right, dims):
+    return mm(jnp.concatenate(left, axis=dims[0][0][0]), jnp.concatenate(right, axis=dims[0][1][0]), dims)
+
+
+def mm3(a, b, dims=NN):
+    return joined((a[0], a[1], a[0]), (b[0], b[0], b[1]), dims)
+
+
+def mm6(a, b, dims=NN):
+    a, b = split3(a), split3(b)
+    return joined((a[0], a[1], a[2], a[0], a[1], a[0]), (b[0], b[0], b[0], b[1], b[1], b[2]), dims)
+
+
+def mm6_rows(a, b, dims=NN):
+    n = a.shape[0]
+    a, b = split3(a), split3(b)
+    p = mm(jnp.concatenate(a, axis=0), b[0], dims)
+    q = mm(jnp.concatenate(a[:2], axis=0), b[1], dims)
+    return p[:n] + (p[n : 2 * n] + q[:n]) + (p[2 * n :] + q[n:] + mm(a[0], b[2], dims))
 
 
 def eye_mask(n):
     return lax.broadcasted_iota(jnp.int32, (n, n), 0) == lax.broadcasted_iota(jnp.int32, (n, n), 1)
 
 
-def inverses(mats):
+def inverses(mats, others=()):
+    others = list(others)
+
+    def between():
+        if others:
+            others.pop(0)()
+
     n = mats[0].shape[0]
     eye = jnp.where(eye_mask(n), 1.0, 0.0).astype(jnp.float32)
     state = []
@@ -55,32 +98,29 @@
         rs = split(r)
         r = (1.0 - gain) * eye + gain * mm3(rs, rs)
         state.append((x, r, err * err * gain * 0.5))
+    between()
     for step in range(JOINT_STEPS + 1):
         later = []
         for x, r, err in state:
             gain = 2.0 / (2.0 - err * err)
             rs = split(r)
-            xs = split(x)
+            x = gain * (x + joined(split(x), (rs[0], rs[0]), NN))
             if step < JOINT_STEPS:
-                left = mm(jnp.concatenate(xs + rs, axis=0), rs[0])
-                square = left[2 * n : 3 * n] + (left[3 * n :] + mm(rs[0], rs[1]))
-                r = (1.0 - gain) * eye + gain * square
-            else:
-                left = mm(jnp.concatenate(xs, axis=0), rs[0])
-            x = gain * (x + (left[:n] + left[n : 2 * n]))
+                r = (1.0 - gain) * eye + gain * mm3(rs, rs)
             later.append((x, r, err * err * gain * 0.5))
         state = later
-    for last in (False, True):
-        later = []
-        for a, (x, r, err) in zip(mats, state):
-            gain = 2.0 / (2.0 - err * err)
-            xs = split(x)
-            r = eye - (mm6(a, x) if last else mm3(split(a), xs))
-            left = mm(jnp.concatenate(xs, axis=0), r.astype(jnp.bfloat16))
-            x = gain * (x + (left[:n] + left[n:]))
-            later.append((x, r, err * err * gain * 0.5))
-        state = later
-    return [s[0] for s in state]
+        between()
+    exact = [eye - mm6(a, s[0]) for a, s in zip(mats, state)]
+    between()
+    mid = []
+    for r, (x, _, _) in zip(exact, state):
+        rs = split(r)
+        mid.append((x + mm3(split(x), rs), mm3(rs, rs)))
+    between()
+    out = [x + mm3(split(x), split(r)) for x, r in mid]
+    while others:
+        between()
+    return out
 
 
 def place():
@@ -146,7 +186,9 @@
     return scratch[...]
 
 
-def own_kernel(picks_ref, own_ref, frames_ref, weights_ref, labels_ref, inv_ref, term_ref, tall_ref, flat_ref, w_scr, l_scr):
+def own_kernel(
+    picks_ref, own_ref, frames_ref, weights_ref, labels_ref, inv_ref, term_ref, tall_ref, flat_ref, w_scr, l_scr
+):
     feats, rows = frames_ref.shape
     half = own_ref.shape[0]
     device, pos, _ = place()
@@ -156,27 +198,37 @@
     inner = [mm(c, c, NT) for c in chosen]
     sums = [diag_sums(g, diag) for g in inner]
     mats = [gauss(t, f, g, feats) + one for (t, f), g in zip(sums, inner)]
-    inv = inverses(mats)
-    for s in range(2):
-        inv_ref[s] = inv[s]
+    for s in range(2):
         flat_ref[s : s + 1, :] = sums[s][1]
         tall_ref[:, s : s + 1] = sums[s][0]
-    frames = frames_ref[...]
-    frame_sq = frame_squares(frames)
-    weights = padded(weights_ref, w_scr)
-    wsplit = split(weights)
-    start = padded(labels_ref, l_scr) - RIDGE * weights
-    hot = onehots(picks_ref, device, rows)
-    here = lax.broadcasted_iota(jnp.int32, (1, half), 1) == pos
-    for s in range(2):
-        picked = jnp.sum(start * hot[s : s + 1], axis=1, keepdims=True)
-        term = term_of(chosen[s], sums[s][0], frames, frame_sq, wsplit, feats)
-        term_ref[s] = jnp.where(here, picked, 0.0) - term
+    kept = {}
+
+    def prepare():
+        kept["frames"] = frames_ref[...]
+        kept["squares"] = frame_squares(kept["frames"])
+        weights = padded(weights_ref, w_scr)
+        kept["weights"] = split(weights)
+        kept["start"] = padded(labels_ref, l_scr) - RIDGE * weights
+        kept["hot"] = onehots(picks_ref, device, rows)
+
+    def term(s):
+        def go():
+            here = lax.broadcasted_iota(jnp.int32, (1, half), 1) == pos
+            picked = jnp.sum(kept["start"] * kept["hot"][s : s + 1], axis=1, keepdims=True)
+            summed = term_of(chosen[s], sums[s][0], kept["frames"], kept["squares"], kept["weights"], feats)
+            term_ref[s] = jnp.where(here, picked, 0.0) - summed
+
+        return go
+
+    inv = inverses(mats, [prepare, term(0), term(1)])
+    for s in range(2):
+        inv_ref[s] = inv[s]
 
 
 def rest_kernel(own_ref, other_ref, frames_ref, weights_ref, inv_ref, term_ref, tall_ref, flat_ref, out_ref, w_scr):
     feats, rows = frames_ref.shape
     half = own_ref.shape[0]
+    width = own_ref.shape[1] // 2
     _, _, core = place()
     near = halves(own_ref, feats)
     far = halves(other_ref, feats)
@@ -191,38 +243,60 @@
     def block(s, i, t, j):
         return gauss(talls[s][i], flats[t][j], mm(chosen[s][i], chosen[t][j], NT), feats)
 
-    inv, couple, lower, upper, schur = [], [], [], [], []
-    for s in range(2):
-        inv.append(inv_ref[s])
-        upper.append(block(s, 0, s, 1))
+    inv = [inv_ref[s] for s in range(2)]
+    upper = [block(s, 0, s, 1) for s in range(2)]
+    lower, couple, schur = [], [], []
+    for s in range(2):
         lower.append(block(s, 1, s, 0))
-        couple.append(mm6(inv[s], upper[s]))
+        couple.append(mm6_rows(inv[s], upper[s]))
+    for s in range(2):
         corner = gauss(talls[s][1], flats[s][1], inner[s], feats) + one
-        schur.append(corner - mm6(lower[s], couple[s]))
-    inv2 = inverses(schur)
-
-    frames = frames_ref[...]
-    frame_sq = frame_squares(frames)
-    wsplit = split(padded(weights_ref, w_scr))
-    width = own_ref.shape[1] // 2
-    flags = [r[:, width + feats : width + feats + 1].astype(jnp.float32) for r in (own_ref, other_ref)]
-    deltas = []
-    for s in range(2):
-        first = term_ref[s]
-        second = -term_of(far[s], talls[s][1], frames, frame_sq, wsplit, feats)
-        if s == 1:
-            cross = [[block(1, i, 0, j) for j in range(2)] for i in range(2)]
-            for i in range(2):
-                cross[i][i] = cross[i][i] + jnp.where(diag, RIDGE * flags[i], 0.0)
-            first = first - (mm6(deltas[0][0], cross[0][0], NT) + mm6(deltas[0][1], cross[0][1], NT))
-            second = second - (mm6(deltas[0][0], cross[1][0], NT) + mm6(deltas[0][1], cross[1][1], NT))
-        y = mm6(first, inv[s])
-        z = mm6(second - mm6(y, upper[s]), inv2[s])
-        deltas.append((y - mm6(z, couple[s], NT), z))
+        schur.append(corner - mm6_rows(lower[s], couple[s]))
+    kept = {}
+
+    def prepare():
+        kept["frames"] = frames_ref[...]
+        kept["squares"] = frame_squares(kept["frames"])
+        kept["weights"] = split(padded(weights_ref, w_scr))
+
+    def term(s):
+        def go():
+            kept["term", s] = -term_of(
+                far[s], talls[s][1], kept["frames"], kept["squares"], kept["weights"], feats
+            )
+
+        return go
+
+    def cross(i):
+        def go():
+            row = [block(1, i, 0, j) for j in range(2)]
+            flag = (own_ref, other_ref)[i][:, width + feats : width + feats + 1].astype(jnp.float32)
+            row[i] = row[i] + jnp.where(diag, RIDGE * flag, 0.0)
+            kept["cross", i] = jnp.concatenate(row, axis=1)
+
+        return go
+
+    def forward(s, first, second):
+        return mm6_rows(first, inv[s]), second - mm6_rows(first, couple[s])
+
+    def early():
+        kept["forward"] = forward(0, term_ref[0], kept["term", 0])
+
+    last = inverses(schur, [prepare, term(0), early, term(1), cross(0), cross(1)])
+
+    def backward(s, y, m):
+        z = mm6_rows(m, last[s])
+        return y - mm6_rows(z, couple[s], NT), z
+
+    deltas = [backward(0, *kept["forward"])]
+    both = jnp.concatenate(deltas[0], axis=1)
+    first = term_ref[1] - mm6_rows(both, kept["cross", 0], NT)
+    second = kept["term", 1] - mm6_rows(both, kept["cross", 1], NT)
+    deltas.append(backward(1, *forward(1, first, second)))
 
     per = 16
     groups = half // per
-    fill = jnp.zeros((2 * LANES - deltas[0][0].shape[0], half), jnp.float32)
+    fill = jnp.zeros((2 * LANES - both.shape[0], half), jnp.float32)
     for i, slot in enumerate((core, 1 - core)):
         packed = None
         for s in range(2):
@@ -306,7 +380,14 @@
 def shards(frames, labels, weights, picks):
     n_xy, n_z, n_core = (lax.axis_size(a) for a in ("xy", "z", "core"))
     frames, labels, weights = frames.T, labels.T, weights.T
-    sent = kernel(pick_kernel, [SMEM, VMEM], jax.ShapeDtypeStruct((n_z, 8, LANES), jnp.bfloat16))(picks, frames)
+    sent = pl.pallas_call(
+        pick_kernel,
+        grid=(1,),
+        in_specs=[SMEM, pl.BlockSpec(frames.shape, lambda i: (0, 0))],
+        out_specs=pl.BlockSpec((n_z, 8, LANES), lambda i: (0, 0, 0)),
+        out_shape=jax.ShapeDtypeStruct((n_z, 8, LANES), jnp.bfloat16),
+        compiler_params=pltpu.CompilerParams(vmem_limit_bytes=60 * 1024 * 1024),
+    )(picks, frames)
     got = lax.all_to_all(sent, "z", 0, 0).reshape(n_z, 8 * LANES)
     got = lax.all_to_all(jnp.broadcast_to(got[None], (n_xy,) + got.shape), "xy", 0, 0)
     got = got.reshape(n_xy * n_z, 8 * LANES)

time: 101 us -> 96.2 us (0.952)
  Pallas kernels: 20.2 us -> 17 us
  local copies, waits for them, and re-layouts: 1.7 us -> 0.08 us
    pallas_call x1, Pallas kernels: 11.5 us -> 8.36 us  [update(): kernel(rest_kernel, [VMEM] * 8, f32(n_xy, 2, 40, LANES), [scratch], flops...]
    unnamed x11 -> x9, local copies, waits for them, and re-layouts: 1.65 us -> 0.03 us
    pallas_call x1, Pallas kernels: 6.33 us -> 5.25 us  [update(): kernel(own_kernel, [SMEM] + [VMEM] * 4, [f32(2, half, half), f32(2, tall,...]
  transfers between devices with their start and end apart: 1 -> 1, of which waited for: 0 -> 0; matrix products, arithmetic and copies ran while one was open for 0% -> 0% of each run, Pallas kernels for 6% -> 5%
where the time goes in v3:
time: 96.2 us; the launch traced here: 95.9 us
  blocking collectives  73.4 us (76%)
  Pallas kernels  17 us (18%)
  starting transfers between devices  5.28 us (5%)
    all_to_all x1, blocking collectives, shards(): got = lax.all_to_all(sent, 'z', 0, 0).reshape(n_z, 8 * LANES)  27.2 us
    all_to_all x1, blocking collectives, shards(): lax.all_to_all(sent.reshape(n_xy * n_core, 40, LANES), ('xy', 'core'), 0, 0)  16.3 us
    all_to_all x1, blocking collectives, shards(): lax.all_to_all(jnp.broadcast_to(got[None], (n_xy,) + got.shape), 'xy', 0, 0)  15.9 us
    all_to_all x1, blocking collectives, shards(): got = lax.all_to_all(part, 'z', 0, 0)  14 us
    pallas_call x1, Pallas kernels, update(): kernel(rest_kernel, [VMEM] * 8, f32(n_xy, 2, 40, LANES), [scratch], flops...  8.36 us
    ppermute x1, starting transfers between devices, shards(): other = lax.ppermute(got, 'core', [(0, 1), (1, 0)])  5.28 us
    pallas_call x1, Pallas kernels, update(): kernel(own_kernel, [SMEM] + [VMEM] * 4, [f32(2, half, half), f32(2, tall,...  5.25 us
  transfers between devices with their start and end apart: 1, of which 0 were waited for; matrix products, arithmetic and copies ran while one was open for 0% of the time, Pallas kernels for 5%

profile of v3, /device:TPU:1, one launch (start us, length us, event | category | flops | bytes accessed | tf_op | source)
XLA Modules:
  0.0 95.9 jit_solution(7187393992838331486)
XLA Ops:
  0.0 1.7 %shard_map.46 = bf16[16,8,128]{2,1,0:T(8,128)(2,1)} custom-call(s32[2,512]{1,0:T(2,128)} %picks_ref.5, bf16[440,256]{1,0:T(8,128)(2,1)} %bitcast.14), custom_call_target="tpu_custom_call" | custom-call | tf_op jit(solution)/shard_map/pallas_call | solution.py:383
  1.8 27.2 %all_to_all.20 = bf16[16,8,128]{2,1,0:T(8,128)(2,1)S(1)} all-to-all(bf16[16,8,128]{2,1,0:T(8,128)(2,1)} %shard_map.46), channel_id=1, replica_groups=mesh['xy'=16,'z'=16,'core'=2] {'z'}, dimensions={0} | all-to-all | bytes 65536 | tf_op jit(solution)/shard_map/all_to_all | solution.py:391
  29.0 0.1 broadcast_in_dim.8
  29.0 0.0 copy-start
  29.0 0.0 copy-start.1
  29.1 0.0 copy-start.3
  29.1 15.9 %all_to_all.21 = bf16[16,16,1024]{2,1,0:T(8,128)(2,1)S(1)} all-to-all(bf16[16,16,1024]{2,1,0:T(8,128)(2,1)S(1)} %broadcast_in_dim.8), channel_id=1, replica_groups=mesh['xy'=16,'z'=16,'core'=2] {'xy'}, dimensions={0} | all-to-all | bytes 1048576 | tf_op jit(solution)/shard_map/all_to_all | solution.py:392
  45.0 0.0 copy-start.2
  45.0 5.3 %collective-permute-start = (bf16[256,1024]{1,0:T(8,128)(2,1)S(1)}, bf16[256,1024]{1,0:T(8,128)(2,1)S(1)}, u32[]{:S(2)}, u32[]{:S(2)}) collective-permute-start(bf16[256,1024]{1,0:T(8,128)(2,1)S(1)} %bitcast.11), channel_id=1, source_target_pairs={{0,1},{1,0},{2,3},{3,2},{4,5},{5,4},{6,7},{7,6},{8,9},{9,8},{10,11... | collective-permute-start | bytes 1572872 | tf_op jit(solution)/shard_map/ppermute | solution.py:394
  50.2 0.0 copy-done
  50.3 0.0 copy-done.1
  50.3 0.0 copy-done.3
  50.3 0.0 copy-done.2
  50.3 5.3 %shard_map.47 = (f32[2,256,256]{2,1,0:T(8,128)S(1)}, f32[2,152,256]{2,1,0:T(8,128)S(1)}, f32[256,2]{1,0:T(8,128)S(1)}, f32[2,256]{1,0:T(2,128)S(1)}) custom-call(s32[2,512]{1,0:T(2,128)S(1)} %copy-done.2, bf16[256,1024]{1,0:T(8,128)(2,1)S(1)} %bitcast.12, bf16[440,256]{1,0:T(8,128)(2,1)S(1)} %bitcast.15, f32[147,256]{1,0:T(8,128)S(1)} %bitcast.17, ...), custom_call_target="tpu_custom_call" | custom-call | flops 6000000000 | bytes 1048576 | tf_op jit(solution)/shard_map/pallas_call | solution.py:368
  55.5 0.0 collective-permute-done.other_ref
  55.6 8.4 %shard_map.48 = f32[16,2,40,128]{3,2,1,0:T(8,128)S(1)} custom-call(bf16[256,1024]{1,0:T(8,128)(2,1)S(1)} %bitcast.13, bf16[256,1024]{1,0:T(8,128)(2,1)S(1)} %collective-permute-done.other_ref, bf16[440,256]{1,0:T(8,128)(2,1)S(1)} %bitcast.16, f32[147,256]{1,0:T(8,128)S(1)} %bitcast.18, f32[2,256,256]{2,1,0:T(8,128)S(1)} %get-tuple-element.9.inv_ref, ...), custom_call_target="tpu_custom_call" | custom-call | flops 6000000000 | bytes 1048576 | tf_op jit(solution)/shard_map/pallas_call | solution.py:375
  63.9 16.3 %all_to_all.22.got_ref = f32[32,40,128]{2,1,0:T(8,128)S(1)} all-to-all(f32[32,40,128]{2,1,0:T(8,128)S(1)} %bitcast.10), channel_id=1, replica_groups=mesh['xy'=16,'z'=16,'core'=2] {'xy','core'}, dimensions={0} | all-to-all | bytes 1310720 | tf_op jit(solution)/shard_map/all_to_all | solution.py:396
  80.3 0.1 shard_map.49
  80.4 14.0 %all_to_all.23.got_ref = f32[16,4,128]{2,1,0:T(4,128)S(1)} all-to-all(f32[16,4,128]{2,1,0:T(4,128)S(1)} %shard_map.49), channel_id=1, replica_groups=mesh['xy'=16,'z'=16,'core'=2] {'z'}, dimensions={0} | all-to-all | bytes 65536 | tf_op jit(solution)/shard_map/all_to_all | solution.py:398
  94.4 1.5 %shard_map.50 = f32[147,256]{1,0:T(8,128)} custom-call(s32[2,512]{1,0:T(2,128)S(1)} %copy-done.2, f32[16,4,128]{2,1,0:T(4,128)S(1)} %all_to_all.23.got_ref, f32[147,256]{1,0:T(8,128)S(1)} %bitcast.19), custom_call_target="tpu_custom_call" | custom-call | bytes 1048576 | tf_op jit(solution)/shard_map/pallas_call | solution.py:399
  (1 shorter events, 0.0 us)
Async XLA Ops:
  29.0 21.2 %copy-start = (bf16[256,440]{0,1:T(8,128)(2,1)S(1)}, bf16[256,440]{0,1:T(8,128)(2,1)}, u32[]{:S(2)}) copy-start(bf16[256,440]{0,1:T(8,128)(2,1)} %param.4) | copy-start | bytes 675844
  29.0 21.2 %copy-start.1 = (f32[256,147]{0,1:T(8,128)S(1)}, f32[256,147]{0,1:T(8,128)}, u32[]{:S(2)}) copy-start(f32[256,147]{0,1:T(8,128)} %param.6) | copy-start | bytes 451588
  29.1 21.2 %copy-start.3 = (bf16[256,147]{0,1:T(8,128)(2,1)S(1)}, bf16[256,147]{0,1:T(8,128)(2,1)}, u32[]{:S(2)}) copy-start(bf16[256,147]{0,1:T(8,128)(2,1)} %param.5) | copy-start | bytes 225796
  45.0 5.3 %copy-start.2 = (s32[2,512]{1,0:T(2,128)S(1)}, s32[2,512]{1,0:T(2,128)}, u32[]{:S(2)}) copy-start(s32[2,512]{1,0:T(2,128)} %picks_ref.5) | copy-start | bytes 12292
  45.0 10.6 %collective-permute-start = (bf16[256,1024]{1,0:T(8,128)(2,1)S(1)}, bf16[256,1024]{1,0:T(8,128)(2,1)S(1)}, u32[]{:S(2)}, u32[]{:S(2)}) collective-permute-start(bf16[256,1024]{1,0:T(8,128)(2,1)S(1)} %bitcast.11), channel_id=1, source_target_pairs={{0,1},{1,0},{2,3},{3,2},{4,5},{5,4},{6,7},{7,6},{8,9},{9,8},{10,11... | collective-permute-start | bytes 1572872 | tf_op jit(solution)/shard_map/ppermute | solution.py:394

commit v4 on v3

--- a/solution.py
+++ b/solution.py
@@ -130,17 +130,18 @@
 
 
 def onehots(picks_ref, device, rows):
-    at = lax.broadcasted_iota(jnp.int32, (8, rows), 1)
-    row = lax.broadcasted_iota(jnp.int32, (8, rows), 0)
-    want = jnp.where(row == 0, picks_ref[0, device], jnp.where(row == 1, picks_ref[1, device], -1))
-    return jnp.where(at == want, 1.0, 0.0)
+    lane = lax.broadcasted_iota(jnp.int32, picks_ref.shape, 1)
+    own = jnp.where(lane == device, picks_ref[...].astype(jnp.float32), 0.0)
+    own = jnp.sum(own, axis=1, keepdims=True).astype(jnp.int32)
+    return jnp.where(lax.broadcasted_iota(jnp.int32, (2, rows), 1) == own, 1.0, 0.0)
 
 
 def pick_kernel(picks_ref, frames_ref, out_ref):
     feats, rows = frames_ref.shape
     device, _, _ = place()
-    chosen = mm(onehots(picks_ref, device, rows).astype(jnp.bfloat16), frames_ref[...], NT)
-    same = jnp.where(picks_ref[0, device] == picks_ref[1, device], 1.0, 0.0)
+    hot = onehots(picks_ref, device, rows)
+    chosen = mm(hot.astype(jnp.bfloat16), frames_ref[...], NT)
+    same = jnp.sum(hot[0:1] * hot[1:2], axis=1, keepdims=True)
     lane = lax.broadcasted_iota(jnp.int32, (1, LANES), 1)
     parts = []
     for s in range(2):
@@ -340,7 +341,6 @@
 
 
 VMEM = pl.BlockSpec(memory_space=pltpu.VMEM)
-SMEM = pl.BlockSpec(memory_space=pltpu.SMEM)
 
 
 def kernel(body, ins, outs, scratch=(), flops=0):
@@ -367,7 +367,7 @@
     scratch = pltpu.VMEM((tall, rows), jnp.float32)
     known = kernel(
         own_kernel,
-        [SMEM] + [VMEM] * 4,
+        [VMEM] * 5,
         [f32(2, half, half), f32(2, tall, half), f32(half, 2), f32(2, half)],
         [scratch, scratch],
         flops=6_000_000_000,
@@ -383,7 +383,7 @@
     sent = pl.pallas_call(
         pick_kernel,
         grid=(1,),
-        in_specs=[SMEM, pl.BlockSpec(frames.shape, lambda i: (0, 0))],
+        in_specs=[pl.BlockSpec(picks.shape, lambda i: (0, 0)), pl.BlockSpec(frames.shape, lambda i: (0, 0))],
         out_specs=pl.BlockSpec((n_z, 8, LANES), lambda i: (0, 0, 0)),
         out_shape=jax.ShapeDtypeStruct((n_z, 8, LANES), jnp.bfloat16),
         compiler_params=pltpu.CompilerParams(vmem_limit_bytes=60 * 1024 * 1024),
@@ -396,7 +396,7 @@
     got = lax.all_to_all(sent.reshape(n_xy * n_core, 40, LANES), ("xy", "core"), 0, 0)
     part = kernel(mid_kernel, [VMEM], f32(n_z, 4, LANES))(got)
     got = lax.all_to_all(part, "z", 0, 0)
-    return kernel(end_kernel, [SMEM, VMEM, VMEM], f32(*weights.shape))(picks, got, weights).T
+    return kernel(end_kernel, [VMEM] * 3, f32(*weights.shape))(picks, got, weights).T
 
 
 def solution(mesh):

time: 96.2 us -> 95.1 us (0.989)
  Pallas kernels: 17 us -> 15.8 us
    pallas_call x3, Pallas kernels: 8.51 us -> 7.36 us  [the longest x1 4.65 us: update(): kernel(own_kernel, [VMEM] * 5, [f32(2, half, half), f32(2, tall, half), f...]
where the time goes in v4:
time: 95.1 us; the launch traced here: 94.7 us
  blocking collectives  73.5 us (77%)
  Pallas kernels  15.8 us (17%)
  starting transfers between devices  5.28 us (6%)
    all_to_all x1, blocking collectives, shards(): got = lax.all_to_all(sent, 'z', 0, 0).reshape(n_z, 8 * LANES)  27.2 us
    all_to_all x1, blocking collectives, shards(): lax.all_to_all(sent.reshape(n_xy * n_core, 40, LANES), ('xy', 'core'), 0, 0)  16.4 us
    all_to_all x1, blocking collectives, shards(): lax.all_to_all(jnp.broadcast_to(got[None], (n_xy,) + got.shape), 'xy', 0, 0)  15.9 us
    all_to_all x1, blocking collectives, shards(): got = lax.all_to_all(part, 'z', 0, 0)  14 us
    pallas_call x1, Pallas kernels, update(): kernel(rest_kernel, [VMEM] * 8, f32(n_xy, 2, 40, LANES), [scratch], flops...  8.35 us
    ppermute x1, starting transfers between devices, shards(): other = lax.ppermute(got, 'core', [(0, 1), (1, 0)])  5.28 us
    pallas_call x1, Pallas kernels, update(): kernel(own_kernel, [VMEM] * 5, [f32(2, half, half), f32(2, tall, half), f...  4.65 us
  transfers between devices with their start and end apart: 1, of which 0 were waited for; matrix products, arithmetic and copies ran while one was open for 0% of the time, Pallas kernels for 5%

profile of v4, /device:TPU:1, one launch (start us, length us, event | category | flops | bytes accessed | tf_op | source)
XLA Modules:
  0.0 94.7 jit_solution(6850461521262495753)
XLA Ops:
  0.0 1.8 %shard_map.46 = bf16[16,8,128]{2,1,0:T(8,128)(2,1)} custom-call(s32[2,512]{1,0:T(2,128)} %picks_ref.5, bf16[440,256]{1,0:T(8,128)(2,1)} %bitcast.14), custom_call_target="tpu_custom_call" | custom-call | tf_op jit(solution)/shard_map/pallas_call | solution.py:383
  1.8 27.2 %all_to_all.20 = bf16[16,8,128]{2,1,0:T(8,128)(2,1)S(1)} all-to-all(bf16[16,8,128]{2,1,0:T(8,128)(2,1)} %shard_map.46), channel_id=1, replica_groups=mesh['xy'=16,'z'=16,'core'=2] {'z'}, dimensions={0} | all-to-all | bytes 65536 | tf_op jit(solution)/shard_map/all_to_all | solution.py:391
  29.0 0.1 broadcast_in_dim.8
  29.1 0.0 copy-start
  29.1 0.0 copy-start.1
  29.1 0.0 copy-start.3
  29.1 15.9 %all_to_all.21 = bf16[16,16,1024]{2,1,0:T(8,128)(2,1)S(1)} all-to-all(bf16[16,16,1024]{2,1,0:T(8,128)(2,1)S(1)} %broadcast_in_dim.8), channel_id=1, replica_groups=mesh['xy'=16,'z'=16,'core'=2] {'xy'}, dimensions={0} | all-to-all | bytes 1048576 | tf_op jit(solution)/shard_map/all_to_all | solution.py:392
  45.0 0.0 copy-start.2
  45.0 5.3 %collective-permute-start = (bf16[256,1024]{1,0:T(8,128)(2,1)S(1)}, bf16[256,1024]{1,0:T(8,128)(2,1)S(1)}, u32[]{:S(2)}, u32[]{:S(2)}) collective-permute-start(bf16[256,1024]{1,0:T(8,128)(2,1)S(1)} %bitcast.11), channel_id=1, source_target_pairs={{0,1},{1,0},{2,3},{3,2},{4,5},{5,4},{6,7},{7,6},{8,9},{9,8},{10,11... | collective-permute-start | bytes 1572872 | tf_op jit(solution)/shard_map/ppermute | solution.py:394
  50.3 0.0 copy-done
  50.3 0.0 copy-done.1
  50.3 0.0 copy-done.3
  50.3 0.0 copy-done.2
  50.3 4.7 %shard_map.47 = (f32[2,256,256]{2,1,0:T(8,128)S(1)}, f32[2,152,256]{2,1,0:T(8,128)S(1)}, f32[256,2]{1,0:T(8,128)S(1)}, f32[2,256]{1,0:T(2,128)S(1)}) custom-call(s32[2,512]{1,0:T(2,128)S(1)} %copy-done.2, bf16[256,1024]{1,0:T(8,128)(2,1)S(1)} %bitcast.12, bf16[440,256]{1,0:T(8,128)(2,1)S(1)} %bitcast.15, f32[147,256]{1,0:T(8,128)S(1)} %bitcast.17, ...), custom_call_target="tpu_custom_call" | custom-call | flops 6000000000 | bytes 1048576 | tf_op jit(solution)/shard_map/pallas_call | solution.py:368
  55.0 0.0 collective-permute-done.other_ref
  55.0 8.4 %shard_map.48 = f32[16,2,40,128]{3,2,1,0:T(8,128)S(1)} custom-call(bf16[256,1024]{1,0:T(8,128)(2,1)S(1)} %bitcast.13, bf16[256,1024]{1,0:T(8,128)(2,1)S(1)} %collective-permute-done.other_ref, bf16[440,256]{1,0:T(8,128)(2,1)S(1)} %bitcast.16, f32[147,256]{1,0:T(8,128)S(1)} %bitcast.18, f32[2,256,256]{2,1,0:T(8,128)S(1)} %get-tuple-element.9.inv_ref, ...), custom_call_target="tpu_custom_call" | custom-call | flops 6000000000 | bytes 1048576 | tf_op jit(solution)/shard_map/pallas_call | solution.py:375
  63.3 16.4 %all_to_all.22.got_ref = f32[32,40,128]{2,1,0:T(8,128)S(1)} all-to-all(f32[32,40,128]{2,1,0:T(8,128)S(1)} %bitcast.10), channel_id=1, replica_groups=mesh['xy'=16,'z'=16,'core'=2] {'xy','core'}, dimensions={0} | all-to-all | bytes 1310720 | tf_op jit(solution)/shard_map/all_to_all | solution.py:396
  79.7 0.1 shard_map.49
  79.8 14.0 %all_to_all.23.got_ref = f32[16,4,128]{2,1,0:T(4,128)S(1)} all-to-all(f32[16,4,128]{2,1,0:T(4,128)S(1)} %shard_map.49), channel_id=1, replica_groups=mesh['xy'=16,'z'=16,'core'=2] {'z'}, dimensions={0} | all-to-all | bytes 65536 | tf_op jit(solution)/shard_map/all_to_all | solution.py:398
  93.8 0.9 shard_map.50
  (1 shorter events, 0.0 us)
Async XLA Ops:
  29.1 21.2 %copy-start = (bf16[256,440]{0,1:T(8,128)(2,1)S(1)}, bf16[256,440]{0,1:T(8,128)(2,1)}, u32[]{:S(2)}) copy-start(bf16[256,440]{0,1:T(8,128)(2,1)} %param.4) | copy-start | bytes 675844
  29.1 21.2 %copy-start.1 = (f32[256,147]{0,1:T(8,128)S(1)}, f32[256,147]{0,1:T(8,128)}, u32[]{:S(2)}) copy-start(f32[256,147]{0,1:T(8,128)} %param.6) | copy-start | bytes 451588
  29.1 21.2 %copy-start.3 = (bf16[256,147]{0,1:T(8,128)(2,1)S(1)}, bf16[256,147]{0,1:T(8,128)(2,1)}, u32[]{:S(2)}) copy-start(bf16[256,147]{0,1:T(8,128)(2,1)} %param.5) | copy-start | bytes 225796
  45.0 5.3 %copy-start.2 = (s32[2,512]{1,0:T(2,128)S(1)}, s32[2,512]{1,0:T(2,128)}, u32[]{:S(2)}) copy-start(s32[2,512]{1,0:T(2,128)} %picks_ref.5) | copy-start | bytes 12292
  45.0 10.0 %collective-permute-start = (bf16[256,1024]{1,0:T(8,128)(2,1)S(1)}, bf16[256,1024]{1,0:T(8,128)(2,1)S(1)}, u32[]{:S(2)}, u32[]{:S(2)}) collective-permute-start(bf16[256,1024]{1,0:T(8,128)(2,1)S(1)} %bitcast.11), channel_id=1, source_target_pairs={{0,1},{1,0},{2,3},{3,2},{4,5},{5,4},{6,7},{7,6},{8,9},{9,8},{10,11... | collective-permute-start | bytes 1572872 | tf_op jit(solution)/shard_map/ppermute | solution.py:394

commit v5 on v4

--- a/solution.py
+++ b/solution.py
@@ -226,11 +226,12 @@
         inv_ref[s] = inv[s]
 
 
-def rest_kernel(own_ref, other_ref, frames_ref, weights_ref, inv_ref, term_ref, tall_ref, flat_ref, out_ref, w_scr):
+def rest_kernel(
+    own_ref, other_ref, frames_ref, weights_ref, inv_ref, term_ref, tall_ref, flat_ref, keep_ref, send_ref, w_scr
+):
     feats, rows = frames_ref.shape
     half = own_ref.shape[0]
     width = own_ref.shape[1] // 2
-    _, _, core = place()
     near = halves(own_ref, feats)
     far = halves(other_ref, feats)
     diag = eye_mask(half)
@@ -298,12 +299,11 @@
     per = 16
     groups = half // per
     fill = jnp.zeros((2 * LANES - both.shape[0], half), jnp.float32)
-    for i, slot in enumerate((core, 1 - core)):
+    for i, out_ref in enumerate((keep_ref, send_ref)):
         packed = None
         for s in range(2):
             full = jnp.concatenate([deltas[s][i], fill], axis=0)
-            body = jnp.transpose(full[:LANES])
-            out_ref[:, pl.ds(slot, 1), s * per : (s + 1) * per, :] = body.reshape(groups, 1, per, LANES)
+            out_ref[:, s * per : (s + 1) * per, :] = jnp.transpose(full[:LANES]).reshape(groups, per, LANES)
             tail = jnp.transpose(full[LANES:]).reshape(groups, 2, 8, LANES)
             for g in range(2):
                 piece = tail[:, g].reshape(groups * 8, LANES)
@@ -311,7 +311,7 @@
                 if turn:
                     piece = pltpu.roll(piece, turn, 1)
                 packed = piece if packed is None else packed + piece
-        out_ref[:, pl.ds(slot, 1), 2 * per :, :] = packed.reshape(groups, 1, 8, LANES)
+        out_ref[:, 2 * per :, :] = packed.reshape(groups, 8, LANES)
 
 
 def mid_kernel(got_ref, out_ref):
@@ -372,13 +372,13 @@
         [scratch, scratch],
         flops=6_000_000_000,
     )(picks, got, frames, weights, labels)
-    return kernel(rest_kernel, [VMEM] * 8, f32(n_xy, 2, 40, LANES), [scratch], flops=6_000_000_000)(
+    return kernel(rest_kernel, [VMEM] * 8, [f32(n_xy, 40, LANES)] * 2, [scratch], flops=6_000_000_000)(
         got, other, frames, weights, *known
     )
 
 
 def shards(frames, labels, weights, picks):
-    n_xy, n_z, n_core = (lax.axis_size(a) for a in ("xy", "z", "core"))
+    n_xy, n_z = lax.axis_size("xy"), lax.axis_size("z")
     frames, labels, weights = frames.T, labels.T, weights.T
     sent = pl.pallas_call(
         pick_kernel,
@@ -392,8 +392,8 @@
     got = lax.all_to_all(jnp.broadcast_to(got[None], (n_xy,) + got.shape), "xy", 0, 0)
     got = got.reshape(n_xy * n_z, 8 * LANES)
     other = lax.ppermute(got, "core", [(0, 1), (1, 0)])
-    sent = update(got, other, frames, weights, labels, picks, n_xy)
-    got = lax.all_to_all(sent.reshape(n_xy * n_core, 40, LANES), ("xy", "core"), 0, 0)
+    keep, send = update(got, other, frames, weights, labels, picks, n_xy)
+    got = lax.all_to_all(keep + lax.ppermute(send, "core", [(0, 1), (1, 0)]), "xy", 0, 0)
     part = kernel(mid_kernel, [VMEM], f32(n_z, 4, LANES))(got)
     got = lax.all_to_all(part, "z", 0, 0)
     return kernel(end_kernel, [VMEM] * 3, f32(*weights.shape))(picks, got, weights).T

time: 95.1 us -> 93.8 us (0.986)
  blocking collectives: 73.5 us -> 68.2 us
  starting transfers between devices: 5.28 us -> 7.2 us
  waiting for transfers between devices: 0.01 us -> 1.59 us
    all_to_all x1, blocking collectives: 16.4 us -> 11.2 us  [shards(): lax.all_to_all(keep + lax.ppermute(send, 'core', [(0, 1), (1, 0)]), 'xy',...]
    ppermute x0 -> x1, starting transfers between devices: none -> 1.93 us  [shards(): lax.ppermute(send, 'core', [(0, 1), (1, 0)])]
    ppermute x0 -> x1, waiting for transfers between devices: none -> 1.59 us  [shards(): lax.ppermute(send, 'core', [(0, 1), (1, 0)])]
  transfers between devices with their start and end apart: 1 -> 2, of which waited for: 0 -> 1; matrix products, arithmetic and copies ran while one was open for 0% -> 0% of each run, Pallas kernels for 5% -> 5%
where the time goes in v5:
time: 93.8 us; the launch traced here: 93 us
  blocking collectives  68.2 us (73%)
  Pallas kernels  15.8 us (17%)
  starting transfers between devices  7.2 us (8%)
  waiting for transfers between devices  1.59 us (2%)
    all_to_all x1, blocking collectives, shards(): got = lax.all_to_all(sent, 'z', 0, 0).reshape(n_z, 8 * LANES)  27.2 us
    all_to_all x1, blocking collectives, shards(): lax.all_to_all(jnp.broadcast_to(got[None], (n_xy,) + got.shape), 'xy', 0, 0)  15.9 us
    all_to_all x1, blocking collectives, shards(): got = lax.all_to_all(part, 'z', 0, 0)  14 us
    all_to_all x1, blocking collectives, shards(): lax.all_to_all(keep + lax.ppermute(send, 'core', [(0, 1), (1, 0)]), 'xy',...  11.2 us
    pallas_call x1, Pallas kernels, update(): kernel(rest_kernel, [VMEM] * 8, [f32(n_xy, 40, LANES)] * 2, [scratch], fl...  8.32 us
    ppermute x1, starting transfers between devices, shards(): other = lax.ppermute(got, 'core', [(0, 1), (1, 0)])  5.28 us
    pallas_call x1, Pallas kernels, update(): kernel(own_kernel, [VMEM] * 5, [f32(2, half, half), f32(2, tall, half), f...  4.65 us
    ppermute x1, starting transfers between devices, shards(): lax.ppermute(send, 'core', [(0, 1), (1, 0)])  1.93 us
  transfers between devices with their start and end apart: 2, of which 1 were waited for; matrix products, arithmetic and copies ran while one was open for 0% of the time, Pallas kernels for 5%

profile of v5, /device:TPU:1, one launch (start us, length us, event | category | flops | bytes accessed | tf_op | source)
XLA Modules:
  0.0 93.0 jit_solution(6630932191990491982)
XLA Ops:
  0.0 1.8 %shard_map.46 = bf16[16,8,128]{2,1,0:T(8,128)(2,1)} custom-call(s32[2,512]{1,0:T(2,128)} %picks_ref.5, bf16[440,256]{1,0:T(8,128)(2,1)} %bitcast.12), custom_call_target="tpu_custom_call" | custom-call | tf_op jit(solution)/shard_map/pallas_call | solution.py:383
  1.8 27.2 %all_to_all.20 = bf16[16,8,128]{2,1,0:T(8,128)(2,1)S(1)} all-to-all(bf16[16,8,128]{2,1,0:T(8,128)(2,1)} %shard_map.46), channel_id=1, replica_groups=mesh['xy'=16,'z'=16,'core'=2] {'z'}, dimensions={0} | all-to-all | bytes 65536 | tf_op jit(solution)/shard_map/all_to_all | solution.py:391
  29.0 0.1 broadcast_in_dim.8
  29.1 0.0 copy-start
  29.1 0.0 copy-start.1
  29.1 0.0 copy-start.3
  29.1 15.9 %all_to_all.21 = bf16[16,16,1024]{2,1,0:T(8,128)(2,1)S(1)} all-to-all(bf16[16,16,1024]{2,1,0:T(8,128)(2,1)S(1)} %broadcast_in_dim.8), channel_id=1, replica_groups=mesh['xy'=16,'z'=16,'core'=2] {'xy'}, dimensions={0} | all-to-all | bytes 1048576 | tf_op jit(solution)/shard_map/all_to_all | solution.py:392
  45.0 0.0 copy-start.2
  45.0 5.3 %collective-permute-start = (bf16[256,1024]{1,0:T(8,128)(2,1)S(1)}, bf16[256,1024]{1,0:T(8,128)(2,1)S(1)}, u32[]{:S(2)}, u32[]{:S(2)}) collective-permute-start(bf16[256,1024]{1,0:T(8,128)(2,1)S(1)} %bitcast.9), channel_id=1, source_target_pairs={{0,1},{1,0},{2,3},{3,2},{4,5},{5,4},{6,7},{7,6},{8,9},{9,8},{10,11... | collective-permute-start | bytes 1572872 | tf_op jit(solution)/shard_map/ppermute | solution.py:394
  50.3 0.0 copy-done
  50.3 0.0 copy-done.1
  50.3 0.0 copy-done.3
  50.3 0.0 copy-done.2
  50.3 4.7 %shard_map.47 = (f32[2,256,256]{2,1,0:T(8,128)S(1)}, f32[2,152,256]{2,1,0:T(8,128)S(1)}, f32[256,2]{1,0:T(8,128)S(1)}, f32[2,256]{1,0:T(2,128)S(1)}) custom-call(s32[2,512]{1,0:T(2,128)S(1)} %copy-done.2, bf16[256,1024]{1,0:T(8,128)(2,1)S(1)} %bitcast.10, bf16[440,256]{1,0:T(8,128)(2,1)S(1)} %bitcast.13, f32[147,256]{1,0:T(8,128)S(1)} %bitcast.15, ...), custom_call_target="tpu_custom_call" | custom-call | flops 6000000000 | bytes 1048576 | tf_op jit(solution)/shard_map/pallas_call | solution.py:368
  55.0 0.0 collective-permute-done.other_ref
  55.0 8.3 %shard_map.48 = (f32[16,40,128]{2,1,0:T(8,128)S(1)}, f32[16,40,128]{2,1,0:T(8,128)S(1)}) custom-call(bf16[256,1024]{1,0:T(8,128)(2,1)S(1)} %bitcast.11, bf16[256,1024]{1,0:T(8,128)(2,1)S(1)} %collective-permute-done.other_ref, bf16[440,256]{1,0:T(8,128)(2,1)S(1)} %bitcast.14, f32[147,256]{1,0:T(8,128)S(1)} %bitcast.16, ...), custom_call_target="tpu_custom_call" | custom-call | flops 6000000000 | bytes 1048576 | tf_op jit(solution)/shard_map/pallas_call | solution.py:375
  63.3 1.9 %collective-permute-start.1 = (f32[16,40,128]{2,1,0:T(8,128)S(1)}, f32[16,40,128]{2,1,0:T(8,128)S(1)}, u32[]{:S(2)}, u32[]{:S(2)}) collective-permute-start(f32[16,40,128]{2,1,0:T(8,128)S(1)} %get-tuple-element.16), channel_id=1, source_target_pairs={{0,1},{1,0},{2,3},{3,2},{4,5},{5,4},{6,7},{7,6},{8,9},{9,8},{10,11... | collective-permute-start | bytes 983048 | tf_op jit(solution)/shard_map/ppermute | solution.py:396
  65.3 1.6 %collective-permute-done.1 = f32[16,40,128]{2,1,0:T(8,128)S(1)} collective-permute-done((f32[16,40,128]{2,1,0:T(8,128)S(1)}, f32[16,40,128]{2,1,0:T(8,128)S(1)}, u32[]{:S(2)}, u32[]{:S(2)}) %collective-permute-start.1) | collective-permute-done | bytes 327712 | tf_op jit(solution)/shard_map/ppermute | solution.py:396
  66.9 11.2 %all_to_all.22.got_ref = f32[16,40,128]{2,1,0:T(8,128)S(1)} all-to-all(f32[16,40,128]{2,1,0:T(8,128)S(1)} %add.3), channel_id=1, replica_groups=mesh['xy'=16,'z'=16,'core'=2] {'xy'}, dimensions={0} | all-to-all | bytes 655360 | tf_op jit(solution)/shard_map/all_to_all | solution.py:396
  78.1 0.1 shard_map.49
  78.1 14.0 %all_to_all.23.got_ref = f32[16,4,128]{2,1,0:T(4,128)S(1)} all-to-all(f32[16,4,128]{2,1,0:T(4,128)S(1)} %shard_map.49), channel_id=1, replica_groups=mesh['xy'=16,'z'=16,'core'=2] {'z'}, dimensions={0} | all-to-all | bytes 65536 | tf_op jit(solution)/shard_map/all_to_all | solution.py:398
  92.1 0.9 shard_map.50
  (2 shorter events, 0.1 us)
Async XLA Ops:
  29.1 21.2 %copy-start = (bf16[256,440]{0,1:T(8,128)(2,1)S(1)}, bf16[256,440]{0,1:T(8,128)(2,1)}, u32[]{:S(2)}) copy-start(bf16[256,440]{0,1:T(8,128)(2,1)} %param.4) | copy-start | bytes 675844
  29.1 21.2 %copy-start.1 = (f32[256,147]{0,1:T(8,128)S(1)}, f32[256,147]{0,1:T(8,128)}, u32[]{:S(2)}) copy-start(f32[256,147]{0,1:T(8,128)} %param.6) | copy-start | bytes 451588
  29.1 21.2 %copy-start.3 = (bf16[256,147]{0,1:T(8,128)(2,1)S(1)}, bf16[256,147]{0,1:T(8,128)(2,1)}, u32[]{:S(2)}) copy-start(bf16[256,147]{0,1:T(8,128)(2,1)} %param.5) | copy-start | bytes 225796
  45.0 5.3 %copy-start.2 = (s32[2,512]{1,0:T(2,128)S(1)}, s32[2,512]{1,0:T(2,128)}, u32[]{:S(2)}) copy-start(s32[2,512]{1,0:T(2,128)} %picks_ref.5) | copy-start | bytes 12292
  45.0 10.0 %collective-permute-start = (bf16[256,1024]{1,0:T(8,128)(2,1)S(1)}, bf16[256,1024]{1,0:T(8,128)(2,1)S(1)}, u32[]{:S(2)}, u32[]{:S(2)}) collective-permute-start(bf16[256,1024]{1,0:T(8,128)(2,1)S(1)} %bitcast.9), channel_id=1, source_target_pairs={{0,1},{1,0},{2,3},{3,2},{4,5},{5,4},{6,7},{7,6},{8,9},{9,8},{10,11... | collective-permute-start | bytes 1572872 | tf_op jit(solution)/shard_map/ppermute | solution.py:394
  63.3 3.5 %collective-permute-start.1 = (f32[16,40,128]{2,1,0:T(8,128)S(1)}, f32[16,40,128]{2,1,0:T(8,128)S(1)}, u32[]{:S(2)}, u32[]{:S(2)}) collective-permute-start(f32[16,40,128]{2,1,0:T(8,128)S(1)} %get-tuple-element.16), channel_id=1, source_target_pairs={{0,1},{1,0},{2,3},{3,2},{4,5},{5,4},{6,7},{7,6},{8,9},{9,8},{10,11... | collective-permute-start | bytes 983048 | tf_op jit(solution)/shard_map/ppermute | solution.py:396

commit v6 on v5

--- a/solution.py
+++ b/solution.py
@@ -227,7 +227,7 @@
 
 
 def rest_kernel(
-    own_ref, other_ref, frames_ref, weights_ref, inv_ref, term_ref, tall_ref, flat_ref, keep_ref, send_ref, w_scr
+    own_ref, other_ref, frames_ref, weights_ref, inv_ref, term_ref, tall_ref, flat_ref, send_ref, part_ref, couple_ref, w_scr
 ):
     feats, rows = frames_ref.shape
     half = own_ref.shape[0]
@@ -286,32 +286,42 @@
 
     last = inverses(schur, [prepare, term(0), early, term(1), cross(0), cross(1)])
 
-    def backward(s, y, m):
-        z = mm6_rows(m, last[s])
-        return y - mm6_rows(z, couple[s], NT), z
-
-    deltas = [backward(0, *kept["forward"])]
-    both = jnp.concatenate(deltas[0], axis=1)
+    y, m = kept["forward"]
+    far0 = mm6_rows(m, last[0])
+    own0 = y - mm6_rows(far0, couple[0], NT)
+    both = jnp.concatenate([own0, far0], axis=1)
     first = term_ref[1] - mm6_rows(both, kept["cross", 0], NT)
     second = kept["term", 1] - mm6_rows(both, kept["cross", 1], NT)
-    deltas.append(backward(1, *forward(1, first, second)))
-
+    y, m = forward(1, first, second)
+    far1 = mm6_rows(m, last[1])
+    pack((far0, far1), send_ref)
+    for i, part in enumerate((own0, y, far1)):
+        part_ref[i] = part
+    couple_ref[...] = couple[1]
+
+
+def pack(deltas, out_ref):
+    rows, half = deltas[0].shape
     per = 16
     groups = half // per
-    fill = jnp.zeros((2 * LANES - both.shape[0], half), jnp.float32)
-    for i, out_ref in enumerate((keep_ref, send_ref)):
-        packed = None
-        for s in range(2):
-            full = jnp.concatenate([deltas[s][i], fill], axis=0)
-            out_ref[:, s * per : (s + 1) * per, :] = jnp.transpose(full[:LANES]).reshape(groups, per, LANES)
-            tail = jnp.transpose(full[LANES:]).reshape(groups, 2, 8, LANES)
-            for g in range(2):
-                piece = tail[:, g].reshape(groups * 8, LANES)
-                turn = (2 * s + g) * 32
-                if turn:
-                    piece = pltpu.roll(piece, turn, 1)
-                packed = piece if packed is None else packed + piece
-        out_ref[:, 2 * per :, :] = packed.reshape(groups, 8, LANES)
+    fill = jnp.zeros((2 * LANES - rows, half), jnp.float32)
+    packed = None
+    for s in range(2):
+        full = jnp.concatenate([deltas[s], fill], axis=0)
+        out_ref[:, s * per : (s + 1) * per, :] = jnp.transpose(full[:LANES]).reshape(groups, per, LANES)
+        tail = jnp.transpose(full[LANES:]).reshape(groups, 2, 8, LANES)
+        for g in range(2):
+            piece = tail[:, g].reshape(groups * 8, LANES)
+            turn = (2 * s + g) * 32
+            if turn:
+                piece = pltpu.roll(piece, turn, 1)
+            packed = piece if packed is None else packed + piece
+    out_ref[:, 2 * per :, :] = packed.reshape(groups, 8, LANES)
+
+
+def finish_kernel(part_ref, couple_ref, keep_ref):
+    own1 = part_ref[1] - mm6_rows(part_ref[2], couple_ref[...], NT)
+    pack((part_ref[0], own1), keep_ref)
 
 
 def mid_kernel(got_ref, out_ref):
@@ -372,9 +382,15 @@
         [scratch, scratch],
         flops=6_000_000_000,
     )(picks, got, frames, weights, labels)
-    return kernel(rest_kernel, [VMEM] * 8, [f32(n_xy, 40, LANES)] * 2, [scratch], flops=6_000_000_000)(
-        got, other, frames, weights, *known
-    )
+    send, part, couple = kernel(
+        rest_kernel,
+        [VMEM] * 8,
+        [f32(n_xy, 40, LANES), f32(3, tall, half), f32(half, half)],
+        [scratch],
+        flops=6_000_000_000,
+    )(got, other, frames, weights, *known)
+    keep = kernel(finish_kernel, [VMEM] * 2, f32(n_xy, 40, LANES), flops=500_000_000)(part, couple)
+    return keep, send
 
 
 def shards(frames, labels, weights, picks):

time: 93.8 us -> 93.5 us (level)
    pallas_call x1 -> x2, Pallas kernels: 8.32 us -> 8.6 us  [the longest x1 8.09 us: update(): kernel(rest_kernel, [VMEM] * 8, [f32(n_xy, 40, LANES), f32(3, tall, half)...]
  transfers between devices with their start and end apart: 2 -> 2, of which waited for: 1 -> 1; matrix products, arithmetic and copies ran while one was open for 0% -> 0% of each run, Pallas kernels for 5% -> 6%
where the time goes in v6:
time: 93.5 us; the launch traced here: 92.8 us
  blocking collectives  68.2 us (73%)
  Pallas kernels  16.1 us (17%)
  starting transfers between devices  7.2 us (8%)
  waiting for transfers between devices  1.08 us (1%)
    all_to_all x1, blocking collectives, shards(): got = lax.all_to_all(sent, 'z', 0, 0).reshape(n_z, 8 * LANES)  27.2 us
    all_to_all x1, blocking collectives, shards(): lax.all_to_all(jnp.broadcast_to(got[None], (n_xy,) + got.shape), 'xy', 0, 0)  15.9 us
    all_to_all x1, blocking collectives, shards(): got = lax.all_to_all(part, 'z', 0, 0)  14 us
    all_to_all x1, blocking collectives, shards(): lax.all_to_all(keep + lax.ppermute(send, 'core', [(0, 1), (1, 0)]), 'xy',...  11.2 us
    pallas_call x1, Pallas kernels, update(): kernel(rest_kernel, [VMEM] * 8, [f32(n_xy, 40, LANES), f32(3, tall, half)...  8.09 us
    ppermute x1, starting transfers between devices, shards(): other = lax.ppermute(got, 'core', [(0, 1), (1, 0)])  5.28 us
    pallas_call x1, Pallas kernels, update(): kernel(own_kernel, [VMEM] * 5, [f32(2, half, half), f32(2, tall, half), f...  4.65 us
    ppermute x1, starting transfers between devices, shards(): lax.ppermute(send, 'core', [(0, 1), (1, 0)])  1.93 us
  transfers between devices with their start and end apart: 2, of which 1 were waited for; matrix products, arithmetic and copies ran while one was open for 0% of the time, Pallas kernels for 6%

profile of v6, /device:TPU:1, one launch (start us, length us, event | category | flops | bytes accessed | tf_op | source)
XLA Modules:
  0.0 92.8 jit_solution(2658273457576414485)
XLA Ops:
  0.0 1.8 %shard_map.46 = bf16[16,8,128]{2,1,0:T(8,128)(2,1)} custom-call(s32[2,512]{1,0:T(2,128)} %picks_ref.5, bf16[440,256]{1,0:T(8,128)(2,1)} %bitcast.12), custom_call_target="tpu_custom_call" | custom-call | tf_op jit(solution)/shard_map/pallas_call | solution.py:399
  1.8 27.2 %all_to_all.20 = bf16[16,8,128]{2,1,0:T(8,128)(2,1)S(1)} all-to-all(bf16[16,8,128]{2,1,0:T(8,128)(2,1)} %shard_map.46), channel_id=1, replica_groups=mesh['xy'=16,'z'=16,'core'=2] {'z'}, dimensions={0} | all-to-all | bytes 65536 | tf_op jit(solution)/shard_map/all_to_all | solution.py:407
  29.0 0.1 broadcast_in_dim.8
  29.1 0.0 copy-start
  29.1 0.0 copy-start.1
  29.1 0.0 copy-start.3
  29.1 15.9 %all_to_all.21 = bf16[16,16,1024]{2,1,0:T(8,128)(2,1)S(1)} all-to-all(bf16[16,16,1024]{2,1,0:T(8,128)(2,1)S(1)} %broadcast_in_dim.8), channel_id=1, replica_groups=mesh['xy'=16,'z'=16,'core'=2] {'xy'}, dimensions={0} | all-to-all | bytes 1048576 | tf_op jit(solution)/shard_map/all_to_all | solution.py:408
  45.0 0.0 copy-start.2
  45.0 5.3 %collective-permute-start = (bf16[256,1024]{1,0:T(8,128)(2,1)S(1)}, bf16[256,1024]{1,0:T(8,128)(2,1)S(1)}, u32[]{:S(2)}, u32[]{:S(2)}) collective-permute-start(bf16[256,1024]{1,0:T(8,128)(2,1)S(1)} %bitcast.9), channel_id=1, source_target_pairs={{0,1},{1,0},{2,3},{3,2},{4,5},{5,4},{6,7},{7,6},{8,9},{9,8},{10,11... | collective-permute-start | bytes 1572872 | tf_op jit(solution)/shard_map/ppermute | solution.py:410
  50.3 0.0 copy-done
  50.3 0.0 copy-done.1
  50.3 0.0 copy-done.3
  50.3 0.0 copy-done.2
  50.3 4.6 %shard_map.47 = (f32[2,256,256]{2,1,0:T(8,128)S(1)}, f32[2,152,256]{2,1,0:T(8,128)S(1)}, f32[256,2]{1,0:T(8,128)S(1)}, f32[2,256]{1,0:T(2,128)S(1)}) custom-call(s32[2,512]{1,0:T(2,128)S(1)} %copy-done.2, bf16[256,1024]{1,0:T(8,128)(2,1)S(1)} %bitcast.10, bf16[440,256]{1,0:T(8,128)(2,1)S(1)} %bitcast.13, f32[147,256]{1,0:T(8,128)S(1)} %bitcast.15, ...), custom_call_target="tpu_custom_call" | custom-call | flops 6000000000 | bytes 1048576 | tf_op jit(solution)/shard_map/pallas_call | solution.py:378
  55.0 0.0 collective-permute-done.other_ref
  55.0 8.1 %shard_map.48 = (f32[16,40,128]{2,1,0:T(8,128)S(1)}, f32[3,152,256]{2,1,0:T(8,128)S(1)}, f32[256,256]{1,0:T(8,128)S(1)}) custom-call(bf16[256,1024]{1,0:T(8,128)(2,1)S(1)} %bitcast.11, bf16[256,1024]{1,0:T(8,128)(2,1)S(1)} %collective-permute-done.other_ref, bf16[440,256]{1,0:T(8,128)(2,1)S(1)} %bitcast.14, f32[147,256]{1,0:T(8,128)S(1)} %bitcast.16, ...), custom_call_target="tpu_custom_call" | custom-call | flops 6000000000 | bytes 1048576 | tf_op jit(solution)/shard_map/pallas_call | solution.py:385
  63.1 1.9 %collective-permute-start.1 = (f32[16,40,128]{2,1,0:T(8,128)S(1)}, f32[16,40,128]{2,1,0:T(8,128)S(1)}, u32[]{:S(2)}, u32[]{:S(2)}) collective-permute-start(f32[16,40,128]{2,1,0:T(8,128)S(1)} %get-tuple-element.18), channel_id=1, source_target_pairs={{0,1},{1,0},{2,3},{3,2},{4,5},{5,4},{6,7},{7,6},{8,9},{9,8},{10,11... | collective-permute-start | bytes 983048 | tf_op jit(solution)/shard_map/ppermute | solution.py:412
  65.0 0.5 shard_map.49
  65.5 1.1 %collective-permute-done.1 = f32[16,40,128]{2,1,0:T(8,128)S(1)} collective-permute-done((f32[16,40,128]{2,1,0:T(8,128)S(1)}, f32[16,40,128]{2,1,0:T(8,128)S(1)}, u32[]{:S(2)}, u32[]{:S(2)}) %collective-permute-start.1) | collective-permute-done | bytes 327712 | tf_op jit(solution)/shard_map/ppermute | solution.py:412
  66.6 11.2 %all_to_all.22.got_ref = f32[16,40,128]{2,1,0:T(8,128)S(1)} all-to-all(f32[16,40,128]{2,1,0:T(8,128)S(1)} %add.3), channel_id=1, replica_groups=mesh['xy'=16,'z'=16,'core'=2] {'xy'}, dimensions={0} | all-to-all | bytes 655360 | tf_op jit(solution)/shard_map/all_to_all | solution.py:412
  77.8 0.1 shard_map.50
  77.9 14.0 %all_to_all.23.got_ref = f32[16,4,128]{2,1,0:T(4,128)S(1)} all-to-all(f32[16,4,128]{2,1,0:T(4,128)S(1)} %shard_map.50), channel_id=1, replica_groups=mesh['xy'=16,'z'=16,'core'=2] {'z'}, dimensions={0} | all-to-all | bytes 65536 | tf_op jit(solution)/shard_map/all_to_all | solution.py:414
  91.9 0.9 shard_map.51
  (2 shorter events, 0.0 us)
Async XLA Ops:
  29.1 21.2 %copy-start = (bf16[256,440]{0,1:T(8,128)(2,1)S(1)}, bf16[256,440]{0,1:T(8,128)(2,1)}, u32[]{:S(2)}) copy-start(bf16[256,440]{0,1:T(8,128)(2,1)} %param.4) | copy-start | bytes 675844
  29.1 21.2 %copy-start.1 = (f32[256,147]{0,1:T(8,128)S(1)}, f32[256,147]{0,1:T(8,128)}, u32[]{:S(2)}) copy-start(f32[256,147]{0,1:T(8,128)} %param.6) | copy-start | bytes 451588
  29.1 21.2 %copy-start.3 = (bf16[256,147]{0,1:T(8,128)(2,1)S(1)}, bf16[256,147]{0,1:T(8,128)(2,1)}, u32[]{:S(2)}) copy-start(bf16[256,147]{0,1:T(8,128)(2,1)} %param.5) | copy-start | bytes 225796
  45.0 5.3 %copy-start.2 = (s32[2,512]{1,0:T(2,128)S(1)}, s32[2,512]{1,0:T(2,128)}, u32[]{:S(2)}) copy-start(s32[2,512]{1,0:T(2,128)} %picks_ref.5) | copy-start | bytes 12292
  45.0 10.0 %collective-permute-start = (bf16[256,1024]{1,0:T(8,128)(2,1)S(1)}, bf16[256,1024]{1,0:T(8,128)(2,1)S(1)}, u32[]{:S(2)}, u32[]{:S(2)}) collective-permute-start(bf16[256,1024]{1,0:T(8,128)(2,1)S(1)} %bitcast.9), channel_id=1, source_target_pairs={{0,1},{1,0},{2,3},{3,2},{4,5},{5,4},{6,7},{7,6},{8,9},{9,8},{10,11... | collective-permute-start | bytes 1572872 | tf_op jit(solution)/shard_map/ppermute | solution.py:410
  63.1 3.5 %collective-permute-start.1 = (f32[16,40,128]{2,1,0:T(8,128)S(1)}, f32[16,40,128]{2,1,0:T(8,128)S(1)}, u32[]{:S(2)}, u32[]{:S(2)}) collective-permute-start(f32[16,40,128]{2,1,0:T(8,128)S(1)} %get-tuple-element.18), channel_id=1, source_target_pairs={{0,1},{1,0},{2,3},{3,2},{4,5},{5,4},{6,7},{7,6},{8,9},{9,8},{10,11... | collective-permute-start | bytes 983048 | tf_op jit(solution)/shard_map/ppermute | solution.py:412

commit v7 on v6

--- a/solution.py
+++ b/solution.py
@@ -110,14 +110,14 @@
             later.append((x, r, err * err * gain * 0.5))
         state = later
         between()
-    exact = [eye - mm6(a, s[0]) for a, s in zip(mats, state)]
+    exact = [eye - mm6(s[0], a) for a, s in zip(mats, state)]
     between()
     mid = []
     for r, (x, _, _) in zip(exact, state):
         rs = split(r)
-        mid.append((x + mm3(split(x), rs), mm3(rs, rs)))
+        mid.append((x + mm3(rs, split(x)), mm(rs[0], rs[0])))
     between()
-    out = [x + mm3(split(x), split(r)) for x, r in mid]
+    out = [x + joined((r.astype(jnp.bfloat16),) * 2, split(x), NN) for x, r in mid]
     while others:
         between()
     return out

time: 93.5 us -> 93.1 us (level)
  transfers between devices with their start and end apart: 2 -> 2, of which waited for: 1 -> 1; matrix products, arithmetic and copies ran while one was open for 0% -> 0% of each run, Pallas kernels for 6% -> 5%
where the time goes in v7:
time: 93.1 us; the launch traced here: 92.3 us
  blocking collectives  68.2 us (73%)
  Pallas kernels  15.6 us (17%)
  starting transfers between devices  7.2 us (8%)
  waiting for transfers between devices  1.08 us (1%)
    all_to_all x1, blocking collectives, shards(): got = lax.all_to_all(sent, 'z', 0, 0).reshape(n_z, 8 * LANES)  27.2 us
    all_to_all x1, blocking collectives, shards(): lax.all_to_all(jnp.broadcast_to(got[None], (n_xy,) + got.shape), 'xy', 0, 0)  15.9 us
    all_to_all x1, blocking collectives, shards(): got = lax.all_to_all(part, 'z', 0, 0)  14 us
    all_to_all x1, blocking collectives, shards(): lax.all_to_all(keep + lax.ppermute(send, 'core', [(0, 1), (1, 0)]), 'xy',...  11.2 us
    pallas_call x1, Pallas kernels, update(): kernel(rest_kernel, [VMEM] * 8, [f32(n_xy, 40, LANES), f32(3, tall, half)...  7.86 us
    ppermute x1, starting transfers between devices, shards(): other = lax.ppermute(got, 'core', [(0, 1), (1, 0)])  5.28 us
    pallas_call x1, Pallas kernels, update(): kernel(own_kernel, [VMEM] * 5, [f32(2, half, half), f32(2, tall, half), f...  4.41 us
    ppermute x1, starting transfers between devices, shards(): lax.ppermute(send, 'core', [(0, 1), (1, 0)])  1.92 us
  transfers between devices with their start and end apart: 2, of which 1 were waited for; matrix products, arithmetic and copies ran while one was open for 0% of the time, Pallas kernels for 5%

profile of v7, /device:TPU:1, one launch (start us, length us, event | category | flops | bytes accessed | tf_op | source)
XLA Modules:
  0.0 92.3 jit_solution(12867279602486986257)
XLA Ops:
  0.0 1.8 %shard_map.46 = bf16[16,8,128]{2,1,0:T(8,128)(2,1)} custom-call(s32[2,512]{1,0:T(2,128)} %picks_ref.5, bf16[440,256]{1,0:T(8,128)(2,1)} %bitcast.12), custom_call_target="tpu_custom_call" | custom-call | tf_op jit(solution)/shard_map/pallas_call | solution.py:399
  1.8 27.2 %all_to_all.20 = bf16[16,8,128]{2,1,0:T(8,128)(2,1)S(1)} all-to-all(bf16[16,8,128]{2,1,0:T(8,128)(2,1)} %shard_map.46), channel_id=1, replica_groups=mesh['xy'=16,'z'=16,'core'=2] {'z'}, dimensions={0} | all-to-all | bytes 65536 | tf_op jit(solution)/shard_map/all_to_all | solution.py:407
  29.0 0.1 broadcast_in_dim.8
  29.1 0.0 copy-start
  29.1 0.0 copy-start.1
  29.1 0.0 copy-start.3
  29.1 15.9 %all_to_all.21 = bf16[16,16,1024]{2,1,0:T(8,128)(2,1)S(1)} all-to-all(bf16[16,16,1024]{2,1,0:T(8,128)(2,1)S(1)} %broadcast_in_dim.8), channel_id=1, replica_groups=mesh['xy'=16,'z'=16,'core'=2] {'xy'}, dimensions={0} | all-to-all | bytes 1048576 | tf_op jit(solution)/shard_map/all_to_all | solution.py:408
  45.0 0.0 copy-start.2
  45.0 5.3 %collective-permute-start = (bf16[256,1024]{1,0:T(8,128)(2,1)S(1)}, bf16[256,1024]{1,0:T(8,128)(2,1)S(1)}, u32[]{:S(2)}, u32[]{:S(2)}) collective-permute-start(bf16[256,1024]{1,0:T(8,128)(2,1)S(1)} %bitcast.9), channel_id=1, source_target_pairs={{0,1},{1,0},{2,3},{3,2},{4,5},{5,4},{6,7},{7,6},{8,9},{9,8},{10,11... | collective-permute-start | bytes 1572872 | tf_op jit(solution)/shard_map/ppermute | solution.py:410
  50.3 0.0 copy-done
  50.3 0.0 copy-done.1
  50.3 0.0 copy-done.3
  50.3 0.0 copy-done.2
  50.3 4.4 %shard_map.47 = (f32[2,256,256]{2,1,0:T(8,128)S(1)}, f32[2,152,256]{2,1,0:T(8,128)S(1)}, f32[256,2]{1,0:T(8,128)S(1)}, f32[2,256]{1,0:T(2,128)S(1)}) custom-call(s32[2,512]{1,0:T(2,128)S(1)} %copy-done.2, bf16[256,1024]{1,0:T(8,128)(2,1)S(1)} %bitcast.10, bf16[440,256]{1,0:T(8,128)(2,1)S(1)} %bitcast.13, f32[147,256]{1,0:T(8,128)S(1)} %bitcast.15, ...), custom_call_target="tpu_custom_call" | custom-call | flops 6000000000 | bytes 1048576 | tf_op jit(solution)/shard_map/pallas_call | solution.py:378
  54.7 0.0 collective-permute-done.other_ref
  54.7 7.9 %shard_map.48 = (f32[16,40,128]{2,1,0:T(8,128)S(1)}, f32[3,152,256]{2,1,0:T(8,128)S(1)}, f32[256,256]{1,0:T(8,128)S(1)}) custom-call(bf16[256,1024]{1,0:T(8,128)(2,1)S(1)} %bitcast.11, bf16[256,1024]{1,0:T(8,128)(2,1)S(1)} %collective-permute-done.other_ref, bf16[440,256]{1,0:T(8,128)(2,1)S(1)} %bitcast.14, f32[147,256]{1,0:T(8,128)S(1)} %bitcast.16, ...), custom_call_target="tpu_custom_call" | custom-call | flops 6000000000 | bytes 1048576 | tf_op jit(solution)/shard_map/pallas_call | solution.py:385
  62.6 1.9 %collective-permute-start.1 = (f32[16,40,128]{2,1,0:T(8,128)S(1)}, f32[16,40,128]{2,1,0:T(8,128)S(1)}, u32[]{:S(2)}, u32[]{:S(2)}) collective-permute-start(f32[16,40,128]{2,1,0:T(8,128)S(1)} %get-tuple-element.18), channel_id=1, source_target_pairs={{0,1},{1,0},{2,3},{3,2},{4,5},{5,4},{6,7},{7,6},{8,9},{9,8},{10,11... | collective-permute-start | bytes 983048 | tf_op jit(solution)/shard_map/ppermute | solution.py:412
  64.5 0.5 shard_map.49
  65.1 1.1 %collective-permute-done.1 = f32[16,40,128]{2,1,0:T(8,128)S(1)} collective-permute-done((f32[16,40,128]{2,1,0:T(8,128)S(1)}, f32[16,40,128]{2,1,0:T(8,128)S(1)}, u32[]{:S(2)}, u32[]{:S(2)}) %collective-permute-start.1) | collective-permute-done | bytes 327712 | tf_op jit(solution)/shard_map/ppermute | solution.py:412
  66.2 11.2 %all_to_all.22.got_ref = f32[16,40,128]{2,1,0:T(8,128)S(1)} all-to-all(f32[16,40,128]{2,1,0:T(8,128)S(1)} %add.3), channel_id=1, replica_groups=mesh['xy'=16,'z'=16,'core'=2] {'xy'}, dimensions={0} | all-to-all | bytes 655360 | tf_op jit(solution)/shard_map/all_to_all | solution.py:412
  77.3 0.1 shard_map.50
  77.4 14.0 %all_to_all.23.got_ref = f32[16,4,128]{2,1,0:T(4,128)S(1)} all-to-all(f32[16,4,128]{2,1,0:T(4,128)S(1)} %shard_map.50), channel_id=1, replica_groups=mesh['xy'=16,'z'=16,'core'=2] {'z'}, dimensions={0} | all-to-all | bytes 65536 | tf_op jit(solution)/shard_map/all_to_all | solution.py:414
  91.4 0.9 %shard_map.51 = f32[147,256]{1,0:T(8,128)} custom-call(s32[2,512]{1,0:T(2,128)S(1)} %copy-done.2, f32[16,4,128]{2,1,0:T(4,128)S(1)} %all_to_all.23.got_ref, f32[147,256]{1,0:T(8,128)S(1)} %bitcast.17), custom_call_target="tpu_custom_call" | custom-call | bytes 1048576 | tf_op jit(solution)/shard_map/pallas_call | solution.py:415
  (2 shorter events, 0.0 us)
Async XLA Ops:
  29.1 21.2 %copy-start = (bf16[256,440]{0,1:T(8,128)(2,1)S(1)}, bf16[256,440]{0,1:T(8,128)(2,1)}, u32[]{:S(2)}) copy-start(bf16[256,440]{0,1:T(8,128)(2,1)} %param.4) | copy-start | bytes 675844
  29.1 21.2 %copy-start.1 = (f32[256,147]{0,1:T(8,128)S(1)}, f32[256,147]{0,1:T(8,128)}, u32[]{:S(2)}) copy-start(f32[256,147]{0,1:T(8,128)} %param.6) | copy-start | bytes 451588
  29.1 21.2 %copy-start.3 = (bf16[256,147]{0,1:T(8,128)(2,1)S(1)}, bf16[256,147]{0,1:T(8,128)(2,1)}, u32[]{:S(2)}) copy-start(bf16[256,147]{0,1:T(8,128)(2,1)} %param.5) | copy-start | bytes 225796
  45.0 5.3 %copy-start.2 = (s32[2,512]{1,0:T(2,128)S(1)}, s32[2,512]{1,0:T(2,128)}, u32[]{:S(2)}) copy-start(s32[2,512]{1,0:T(2,128)} %picks_ref.5) | copy-start | bytes 12292
  45.0 9.7 %collective-permute-start = (bf16[256,1024]{1,0:T(8,128)(2,1)S(1)}, bf16[256,1024]{1,0:T(8,128)(2,1)S(1)}, u32[]{:S(2)}, u32[]{:S(2)}) collective-permute-start(bf16[256,1024]{1,0:T(8,128)(2,1)S(1)} %bitcast.9), channel_id=1, source_target_pairs={{0,1},{1,0},{2,3},{3,2},{4,5},{5,4},{6,7},{7,6},{8,9},{9,8},{10,11... | collective-permute-start | bytes 1572872 | tf_op jit(solution)/shard_map/ppermute | solution.py:410
  62.6 3.5 %collective-permute-start.1 = (f32[16,40,128]{2,1,0:T(8,128)S(1)}, f32[16,40,128]{2,1,0:T(8,128)S(1)}, u32[]{:S(2)}, u32[]{:S(2)}) collective-permute-start(f32[16,40,128]{2,1,0:T(8,128)S(1)} %get-tuple-element.18), channel_id=1, source_target_pairs={{0,1},{1,0},{2,3},{3,2},{4,5},{5,4},{6,7},{7,6},{8,9},{9,8},{10,11... | collective-permute-start | bytes 983048 | tf_op jit(solution)/shard_map/ppermute | solution.py:412

commit v8 on v7

--- a/solution.py
+++ b/solution.py
@@ -142,24 +142,25 @@
     hot = onehots(picks_ref, device, rows)
     chosen = mm(hot.astype(jnp.bfloat16), frames_ref[...], NT)
     same = jnp.sum(hot[0:1] * hot[1:2], axis=1, keepdims=True)
+    parts = []
+    full = feats // LANES * LANES
+    for s in range(2):
+        parts += [chosen[s : s + 1, lo : lo + LANES] for lo in range(0, full, LANES)]
+    gap = jnp.zeros((1, LANES // 2 - (feats - full)), jnp.float32)
+    shared = jnp.concatenate([chosen[0:1, full:], gap, chosen[1:2, full:], gap], axis=1)
     lane = lax.broadcasted_iota(jnp.int32, (1, LANES), 1)
-    parts = []
-    for s in range(2):
-        for c in range(4):
-            lo = c * LANES
-            wide = min(LANES, feats - lo)
-            piece = chosen[s : s + 1, lo : lo + wide]
-            if wide < LANES:
-                piece = jnp.concatenate([piece, jnp.zeros((1, LANES - wide), jnp.float32)], axis=1)
-                piece = jnp.where(lane == wide, same, piece)
-            parts.append(piece)
+    parts += [jnp.where(lane == LANES - 1, same, shared), jnp.zeros((1, LANES), jnp.float32)]
     row = jnp.concatenate(parts, axis=0).astype(jnp.bfloat16)
     out_ref[...] = jnp.broadcast_to(row[None], out_ref.shape)
 
 
 def halves(ref, feats):
-    width = ref.shape[1] // 2
-    return [ref[:, s * width : s * width + feats] for s in range(2)]
+    full = feats // LANES * LANES
+    out = []
+    for s in range(2):
+        last = 2 * full + s * (LANES // 2)
+        out.append(jnp.concatenate([ref[:, s * full : (s + 1) * full], ref[:, last : last + feats - full]], axis=1))
+    return out
 
 
 def gauss(tall, flat, inner, feats):
@@ -231,7 +232,6 @@
 ):
     feats, rows = frames_ref.shape
     half = own_ref.shape[0]
-    width = own_ref.shape[1] // 2
     near = halves(own_ref, feats)
     far = halves(other_ref, feats)
     diag = eye_mask(half)
@@ -272,7 +272,7 @@
     def cross(i):
         def go():
             row = [block(1, i, 0, j) for j in range(2)]
-            flag = (own_ref, other_ref)[i][:, width + feats : width + feats + 1].astype(jnp.float32)
+            flag = (own_ref, other_ref)[i][:, -1:].astype(jnp.float32)
             row[i] = row[i] + jnp.where(diag, RIDGE * flag, 0.0)
             kept["cross", i] = jnp.concatenate(row, axis=1)
 
@@ -404,9 +404,9 @@
         out_shape=jax.ShapeDtypeStruct((n_z, 8, LANES), jnp.bfloat16),
         compiler_params=pltpu.CompilerParams(vmem_limit_bytes=60 * 1024 * 1024),
     )(picks, frames)
-    got = lax.all_to_all(sent, "z", 0, 0).reshape(n_z, 8 * LANES)
+    got = lax.all_to_all(sent, "z", 0, 0).reshape(n_z, 8 * LANES)[:, : 7 * LANES]
     got = lax.all_to_all(jnp.broadcast_to(got[None], (n_xy,) + got.shape), "xy", 0, 0)
-    got = got.reshape(n_xy * n_z, 8 * LANES)
+    got = got.reshape(n_xy * n_z, 7 * LANES)
     other = lax.ppermute(got, "core", [(0, 1), (1, 0)])
     keep, send = update(got, other, frames, weights, labels, picks, n_xy)
     got = lax.all_to_all(keep + lax.ppermute(send, "core", [(0, 1), (1, 0)]), "xy", 0, 0)

time: 93.1 us -> 92.9 us (level)
  no operation moved by 1% of the time
where the time goes in v8:
time: 92.9 us; the launch traced here: 92.1 us
  blocking collectives  67.9 us (73%)
  Pallas kernels  15.8 us (17%)
  starting transfers between devices  7.15 us (8%)
  waiting for transfers between devices  1.08 us (1%)
    all_to_all x1, blocking collectives, shards(): got = lax.all_to_all(sent, 'z', 0, 0).reshape(n_z, 8 * LANES)[:, :7 * LANES]  27.2 us
    all_to_all x1, blocking collectives, shards(): lax.all_to_all(jnp.broadcast_to(got[None], (n_xy,) + got.shape), 'xy', 0, 0)  15.6 us
    all_to_all x1, blocking collectives, shards(): got = lax.all_to_all(part, 'z', 0, 0)  14 us
    all_to_all x1, blocking collectives, shards(): lax.all_to_all(keep + lax.ppermute(send, 'core', [(0, 1), (1, 0)]), 'xy',...  11.2 us
    pallas_call x1, Pallas kernels, update(): kernel(rest_kernel, [VMEM] * 8, [f32(n_xy, 40, LANES), f32(3, tall, half)...  7.97 us
    ppermute x1, starting transfers between devices, shards(): other = lax.ppermute(got, 'core', [(0, 1), (1, 0)])  5.23 us
    pallas_call x1, Pallas kernels, update(): kernel(own_kernel, [VMEM] * 5, [f32(2, half, half), f32(2, tall, half), f...  4.42 us
    ppermute x1, starting transfers between devices, shards(): lax.ppermute(send, 'core', [(0, 1), (1, 0)])  1.92 us
  transfers between devices with their start and end apart: 2, of which 1 were waited for; matrix products, arithmetic and copies ran while one was open for 0% of the time, Pallas kernels for 5%

profile of v8, /device:TPU:1, one launch (start us, length us, event | category | flops | bytes accessed | tf_op | source)
XLA Modules:
  0.0 92.1 jit_solution(14110227370588190153)
XLA Ops:
  0.0 1.9 %shard_map.46 = bf16[16,8,128]{2,1,0:T(8,128)(2,1)} custom-call(s32[2,512]{1,0:T(2,128)} %picks_ref.5, bf16[440,256]{1,0:T(8,128)(2,1)} %bitcast.12), custom_call_target="tpu_custom_call" | custom-call | tf_op jit(solution)/shard_map/pallas_call | solution.py:399
  1.9 27.2 %all_to_all.20 = bf16[16,8,128]{2,1,0:T(8,128)(2,1)S(1)} all-to-all(bf16[16,8,128]{2,1,0:T(8,128)(2,1)} %shard_map.46), channel_id=1, replica_groups=mesh['xy'=16,'z'=16,'core'=2] {'z'}, dimensions={0} | all-to-all | bytes 65536 | tf_op jit(solution)/shard_map/all_to_all | solution.py:407
  29.1 0.0 copy-start
  29.1 0.0 copy-start.1
  29.2 0.0 copy-start.3
  29.2 15.6 %all_to_all.21 = bf16[16,16,896]{2,1,0:T(8,128)(2,1)S(1)} all-to-all(bf16[16,16,896]{2,1,0:T(8,128)(2,1)S(1)} %broadcast_in_dim.2), channel_id=1, replica_groups=mesh['xy'=16,'z'=16,'core'=2] {'xy'}, dimensions={0} | all-to-all | bytes 917504 | tf_op jit(solution)/shard_map/all_to_all | solution.py:408
  44.7 0.0 copy-start.2
  44.7 5.2 %collective-permute-start = (bf16[256,896]{1,0:T(8,128)(2,1)S(1)}, bf16[256,896]{1,0:T(8,128)(2,1)S(1)}, u32[]{:S(2)}, u32[]{:S(2)}) collective-permute-start(bf16[256,896]{1,0:T(8,128)(2,1)S(1)} %bitcast.9), channel_id=1, source_target_pairs={{0,1},{1,0},{2,3},{3,2},{4,5},{5,4},{6,7},{7,6},{8,9},{9,8},{10,11... | collective-permute-start | bytes 1376264 | tf_op jit(solution)/shard_map/ppermute | solution.py:410
  50.0 0.0 copy-done
  50.0 0.0 copy-done.1
  50.0 0.0 copy-done.3
  50.0 0.0 copy-done.2
  50.0 4.4 %shard_map.47 = (f32[2,256,256]{2,1,0:T(8,128)S(1)}, f32[2,152,256]{2,1,0:T(8,128)S(1)}, f32[256,2]{1,0:T(8,128)S(1)}, f32[2,256]{1,0:T(2,128)S(1)}) custom-call(s32[2,512]{1,0:T(2,128)S(1)} %copy-done.2, bf16[256,896]{1,0:T(8,128)(2,1)S(1)} %bitcast.10, bf16[440,256]{1,0:T(8,128)(2,1)S(1)} %bitcast.13, f32[147,256]{1,0:T(8,128)S(1)} %bitcast.15, ...), custom_call_target="tpu_custom_call" | custom-call | flops 6000000000 | bytes 1048576 | tf_op jit(solution)/shard_map/pallas_call | solution.py:378
  54.4 0.0 collective-permute-done.other_ref
  54.4 8.0 %shard_map.48 = (f32[16,40,128]{2,1,0:T(8,128)S(1)}, f32[3,152,256]{2,1,0:T(8,128)S(1)}, f32[256,256]{1,0:T(8,128)S(1)}) custom-call(bf16[256,896]{1,0:T(8,128)(2,1)S(1)} %bitcast.11, bf16[256,896]{1,0:T(8,128)(2,1)S(1)} %collective-permute-done.other_ref, bf16[440,256]{1,0:T(8,128)(2,1)S(1)} %bitcast.14, f32[147,256]{1,0:T(8,128)S(1)} %bitcast.16, ...), custom_call_target="tpu_custom_call" | custom-call | flops 6000000000 | bytes 1048576 | tf_op jit(solution)/shard_map/pallas_call | solution.py:385
  62.4 1.9 %collective-permute-start.1 = (f32[16,40,128]{2,1,0:T(8,128)S(1)}, f32[16,40,128]{2,1,0:T(8,128)S(1)}, u32[]{:S(2)}, u32[]{:S(2)}) collective-permute-start(f32[16,40,128]{2,1,0:T(8,128)S(1)} %get-tuple-element.18), channel_id=1, source_target_pairs={{0,1},{1,0},{2,3},{3,2},{4,5},{5,4},{6,7},{7,6},{8,9},{9,8},{10,11... | collective-permute-start | bytes 983048 | tf_op jit(solution)/shard_map/ppermute | solution.py:412
  64.3 0.5 shard_map.49
  64.9 1.1 %collective-permute-done.1 = f32[16,40,128]{2,1,0:T(8,128)S(1)} collective-permute-done((f32[16,40,128]{2,1,0:T(8,128)S(1)}, f32[16,40,128]{2,1,0:T(8,128)S(1)}, u32[]{:S(2)}, u32[]{:S(2)}) %collective-permute-start.1) | collective-permute-done | bytes 327712 | tf_op jit(solution)/shard_map/ppermute | solution.py:412
  66.0 11.2 %all_to_all.22.got_ref = f32[16,40,128]{2,1,0:T(8,128)S(1)} all-to-all(f32[16,40,128]{2,1,0:T(8,128)S(1)} %add.3), channel_id=1, replica_groups=mesh['xy'=16,'z'=16,'core'=2] {'xy'}, dimensions={0} | all-to-all | bytes 655360 | tf_op jit(solution)/shard_map/all_to_all | solution.py:412
  77.1 0.1 shard_map.50
  77.2 14.0 %all_to_all.23.got_ref = f32[16,4,128]{2,1,0:T(4,128)S(1)} all-to-all(f32[16,4,128]{2,1,0:T(4,128)S(1)} %shard_map.50), channel_id=1, replica_groups=mesh['xy'=16,'z'=16,'core'=2] {'z'}, dimensions={0} | all-to-all | bytes 65536 | tf_op jit(solution)/shard_map/all_to_all | solution.py:414
  91.2 0.9 %shard_map.51 = f32[147,256]{1,0:T(8,128)} custom-call(s32[2,512]{1,0:T(2,128)S(1)} %copy-done.2, f32[16,4,128]{2,1,0:T(4,128)S(1)} %all_to_all.23.got_ref, f32[147,256]{1,0:T(8,128)S(1)} %bitcast.17), custom_call_target="tpu_custom_call" | custom-call | bytes 1048576 | tf_op jit(solution)/shard_map/pallas_call | solution.py:415
  (4 shorter events, 0.1 us)
Async XLA Ops:
  29.1 20.8 %copy-start = (bf16[256,440]{0,1:T(8,128)(2,1)S(1)}, bf16[256,440]{0,1:T(8,128)(2,1)}, u32[]{:S(2)}) copy-start(bf16[256,440]{0,1:T(8,128)(2,1)} %param.4) | copy-start | bytes 675844
  29.1 20.8 %copy-start.1 = (f32[256,147]{0,1:T(8,128)S(1)}, f32[256,147]{0,1:T(8,128)}, u32[]{:S(2)}) copy-start(f32[256,147]{0,1:T(8,128)} %param.6) | copy-start | bytes 451588
  29.2 20.8 %copy-start.3 = (bf16[256,147]{0,1:T(8,128)(2,1)S(1)}, bf16[256,147]{0,1:T(8,128)(2,1)}, u32[]{:S(2)}) copy-start(bf16[256,147]{0,1:T(8,128)(2,1)} %param.5) | copy-start | bytes 225796
  44.7 5.3 %copy-start.2 = (s32[2,512]{1,0:T(2,128)S(1)}, s32[2,512]{1,0:T(2,128)}, u32[]{:S(2)}) copy-start(s32[2,512]{1,0:T(2,128)} %picks_ref.5) | copy-start | bytes 12292
  44.7 9.7 %collective-permute-start = (bf16[256,896]{1,0:T(8,128)(2,1)S(1)}, bf16[256,896]{1,0:T(8,128)(2,1)S(1)}, u32[]{:S(2)}, u32[]{:S(2)}) collective-permute-start(bf16[256,896]{1,0:T(8,128)(2,1)S(1)} %bitcast.9), channel_id=1, source_target_pairs={{0,1},{1,0},{2,3},{3,2},{4,5},{5,4},{6,7},{7,6},{8,9},{9,8},{10,11... | collective-permute-start | bytes 1376264 | tf_op jit(solution)/shard_map/ppermute | solution.py:410
  62.4 3.5 %collective-permute-start.1 = (f32[16,40,128]{2,1,0:T(8,128)S(1)}, f32[16,40,128]{2,1,0:T(8,128)S(1)}, u32[]{:S(2)}, u32[]{:S(2)}) collective-permute-start(f32[16,40,128]{2,1,0:T(8,128)S(1)} %get-tuple-element.18), channel_id=1, source_target_pairs={{0,1},{1,0},{2,3},{3,2},{4,5},{5,4},{6,7},{7,6},{8,9},{9,8},{10,11... | collective-permute-start | bytes 983048 | tf_op jit(solution)/shard_map/ppermute | solution.py:412

commit v9 on v7

--- a/solution.py
+++ b/solution.py
@@ -247,13 +247,12 @@
 
     inv = [inv_ref[s] for s in range(2)]
     upper = [block(s, 0, s, 1) for s in range(2)]
-    lower, couple, schur = [], [], []
-    for s in range(2):
-        lower.append(block(s, 1, s, 0))
+    couple, schur = [], []
+    for s in range(2):
         couple.append(mm6_rows(inv[s], upper[s]))
     for s in range(2):
         corner = gauss(talls[s][1], flats[s][1], inner[s], feats) + one
-        schur.append(corner - mm6_rows(lower[s], couple[s]))
+        schur.append(corner - mm6_rows(jnp.transpose(upper[s]), couple[s]))
     kept = {}
 
     def prepare():

time: 93.1 us -> 93 us (level)
  no operation moved by 1% of the time
where the time goes in v9:
time: 93 us; the launch traced here: 92.3 us
  blocking collectives  68.2 us (73%)
  Pallas kernels  15.5 us (17%)
  starting transfers between devices  7.2 us (8%)
  waiting for transfers between devices  1.08 us (1%)
    all_to_all x1, blocking collectives, shards(): got = lax.all_to_all(sent, 'z', 0, 0).reshape(n_z, 8 * LANES)  27.2 us
    all_to_all x1, blocking collectives, shards(): lax.all_to_all(jnp.broadcast_to(got[None], (n_xy,) + got.shape), 'xy', 0, 0)  15.9 us
    all_to_all x1, blocking collectives, shards(): got = lax.all_to_all(part, 'z', 0, 0)  14 us
    all_to_all x1, blocking collectives, shards(): lax.all_to_all(keep + lax.ppermute(send, 'core', [(0, 1), (1, 0)]), 'xy',...  11.2 us
    pallas_call x1, Pallas kernels, update(): kernel(rest_kernel, [VMEM] * 8, [f32(n_xy, 40, LANES), f32(3, tall, half)...  7.81 us
    ppermute x1, starting transfers between devices, shards(): other = lax.ppermute(got, 'core', [(0, 1), (1, 0)])  5.28 us
    pallas_call x1, Pallas kernels, update(): kernel(own_kernel, [VMEM] * 5, [f32(2, half, half), f32(2, tall, half), f...  4.41 us
    ppermute x1, starting transfers between devices, shards(): lax.ppermute(send, 'core', [(0, 1), (1, 0)])  1.92 us
  transfers between devices with their start and end apart: 2, of which 1 were waited for; matrix products, arithmetic and copies ran while one was open for 0% of the time, Pallas kernels for 5%

profile of v9, /device:TPU:1, one launch (start us, length us, event | category | flops | bytes accessed | tf_op | source)
XLA Modules:
  0.0 92.3 jit_solution(638422230300664652)
XLA Ops:
  0.0 1.8 %shard_map.46 = bf16[16,8,128]{2,1,0:T(8,128)(2,1)} custom-call(s32[2,512]{1,0:T(2,128)} %picks_ref.5, bf16[440,256]{1,0:T(8,128)(2,1)} %bitcast.12), custom_call_target="tpu_custom_call" | custom-call | tf_op jit(solution)/shard_map/pallas_call | solution.py:398
  1.8 27.2 %all_to_all.20 = bf16[16,8,128]{2,1,0:T(8,128)(2,1)S(1)} all-to-all(bf16[16,8,128]{2,1,0:T(8,128)(2,1)} %shard_map.46), channel_id=1, replica_groups=mesh['xy'=16,'z'=16,'core'=2] {'z'}, dimensions={0} | all-to-all | bytes 65536 | tf_op jit(solution)/shard_map/all_to_all | solution.py:406
  29.0 0.1 broadcast_in_dim.8
  29.1 0.0 copy-start
  29.1 0.0 copy-start.1
  29.1 0.0 copy-start.3
  29.1 15.9 %all_to_all.21 = bf16[16,16,1024]{2,1,0:T(8,128)(2,1)S(1)} all-to-all(bf16[16,16,1024]{2,1,0:T(8,128)(2,1)S(1)} %broadcast_in_dim.8), channel_id=1, replica_groups=mesh['xy'=16,'z'=16,'core'=2] {'xy'}, dimensions={0} | all-to-all | bytes 1048576 | tf_op jit(solution)/shard_map/all_to_all | solution.py:407
  45.0 0.0 copy-start.2
  45.0 5.3 %collective-permute-start = (bf16[256,1024]{1,0:T(8,128)(2,1)S(1)}, bf16[256,1024]{1,0:T(8,128)(2,1)S(1)}, u32[]{:S(2)}, u32[]{:S(2)}) collective-permute-start(bf16[256,1024]{1,0:T(8,128)(2,1)S(1)} %bitcast.9), channel_id=1, source_target_pairs={{0,1},{1,0},{2,3},{3,2},{4,5},{5,4},{6,7},{7,6},{8,9},{9,8},{10,11... | collective-permute-start | bytes 1572872 | tf_op jit(solution)/shard_map/ppermute | solution.py:409
  50.3 0.0 copy-done
  50.3 0.0 copy-done.1
  50.3 0.0 copy-done.3
  50.3 0.0 copy-done.2
  50.3 4.4 %shard_map.47 = (f32[2,256,256]{2,1,0:T(8,128)S(1)}, f32[2,152,256]{2,1,0:T(8,128)S(1)}, f32[256,2]{1,0:T(8,128)S(1)}, f32[2,256]{1,0:T(2,128)S(1)}) custom-call(s32[2,512]{1,0:T(2,128)S(1)} %copy-done.2, bf16[256,1024]{1,0:T(8,128)(2,1)S(1)} %bitcast.10, bf16[440,256]{1,0:T(8,128)(2,1)S(1)} %bitcast.13, f32[147,256]{1,0:T(8,128)S(1)} %bitcast.15, ...), custom_call_target="tpu_custom_call" | custom-call | flops 6000000000 | bytes 1048576 | tf_op jit(solution)/shard_map/pallas_call | solution.py:377
  54.7 0.0 collective-permute-done.other_ref
  54.7 7.8 %shard_map.48 = (f32[16,40,128]{2,1,0:T(8,128)S(1)}, f32[3,152,256]{2,1,0:T(8,128)S(1)}, f32[256,256]{1,0:T(8,128)S(1)}) custom-call(bf16[256,1024]{1,0:T(8,128)(2,1)S(1)} %bitcast.11, bf16[256,1024]{1,0:T(8,128)(2,1)S(1)} %collective-permute-done.other_ref, bf16[440,256]{1,0:T(8,128)(2,1)S(1)} %bitcast.14, f32[147,256]{1,0:T(8,128)S(1)} %bitcast.16, ...), custom_call_target="tpu_custom_call" | custom-call | flops 6000000000 | bytes 1048576 | tf_op jit(solution)/shard_map/pallas_call | solution.py:384
  62.6 1.9 %collective-permute-start.1 = (f32[16,40,128]{2,1,0:T(8,128)S(1)}, f32[16,40,128]{2,1,0:T(8,128)S(1)}, u32[]{:S(2)}, u32[]{:S(2)}) collective-permute-start(f32[16,40,128]{2,1,0:T(8,128)S(1)} %get-tuple-element.18), channel_id=1, source_target_pairs={{0,1},{1,0},{2,3},{3,2},{4,5},{5,4},{6,7},{7,6},{8,9},{9,8},{10,11... | collective-permute-start | bytes 983048 | tf_op jit(solution)/shard_map/ppermute | solution.py:411
  64.5 0.5 shard_map.49
  65.0 1.1 %collective-permute-done.1 = f32[16,40,128]{2,1,0:T(8,128)S(1)} collective-permute-done((f32[16,40,128]{2,1,0:T(8,128)S(1)}, f32[16,40,128]{2,1,0:T(8,128)S(1)}, u32[]{:S(2)}, u32[]{:S(2)}) %collective-permute-start.1) | collective-permute-done | bytes 327712 | tf_op jit(solution)/shard_map/ppermute | solution.py:411
  66.1 11.2 %all_to_all.22.got_ref = f32[16,40,128]{2,1,0:T(8,128)S(1)} all-to-all(f32[16,40,128]{2,1,0:T(8,128)S(1)} %add.3), channel_id=1, replica_groups=mesh['xy'=16,'z'=16,'core'=2] {'xy'}, dimensions={0} | all-to-all | bytes 655360 | tf_op jit(solution)/shard_map/all_to_all | solution.py:411
  77.3 0.1 shard_map.50
  77.4 14.0 %all_to_all.23.got_ref = f32[16,4,128]{2,1,0:T(4,128)S(1)} all-to-all(f32[16,4,128]{2,1,0:T(4,128)S(1)} %shard_map.50), channel_id=1, replica_groups=mesh['xy'=16,'z'=16,'core'=2] {'z'}, dimensions={0} | all-to-all | bytes 65536 | tf_op jit(solution)/shard_map/all_to_all | solution.py:413
  91.3 0.9 %shard_map.51 = f32[147,256]{1,0:T(8,128)} custom-call(s32[2,512]{1,0:T(2,128)S(1)} %copy-done.2, f32[16,4,128]{2,1,0:T(4,128)S(1)} %all_to_all.23.got_ref, f32[147,256]{1,0:T(8,128)S(1)} %bitcast.17), custom_call_target="tpu_custom_call" | custom-call | bytes 1048576 | tf_op jit(solution)/shard_map/pallas_call | solution.py:414
  (2 shorter events, 0.0 us)
Async XLA Ops:
  29.1 21.2 %copy-start = (bf16[256,440]{0,1:T(8,128)(2,1)S(1)}, bf16[256,440]{0,1:T(8,128)(2,1)}, u32[]{:S(2)}) copy-start(bf16[256,440]{0,1:T(8,128)(2,1)} %param.4) | copy-start | bytes 675844
  29.1 21.2 %copy-start.1 = (f32[256,147]{0,1:T(8,128)S(1)}, f32[256,147]{0,1:T(8,128)}, u32[]{:S(2)}) copy-start(f32[256,147]{0,1:T(8,128)} %param.6) | copy-start | bytes 451588
  29.1 21.2 %copy-start.3 = (bf16[256,147]{0,1:T(8,128)(2,1)S(1)}, bf16[256,147]{0,1:T(8,128)(2,1)}, u32[]{:S(2)}) copy-start(bf16[256,147]{0,1:T(8,128)(2,1)} %param.5) | copy-start | bytes 225796
  45.0 5.3 %copy-start.2 = (s32[2,512]{1,0:T(2,128)S(1)}, s32[2,512]{1,0:T(2,128)}, u32[]{:S(2)}) copy-start(s32[2,512]{1,0:T(2,128)} %picks_ref.5) | copy-start | bytes 12292
  45.0 9.7 %collective-permute-start = (bf16[256,1024]{1,0:T(8,128)(2,1)S(1)}, bf16[256,1024]{1,0:T(8,128)(2,1)S(1)}, u32[]{:S(2)}, u32[]{:S(2)}) collective-permute-start(bf16[256,1024]{1,0:T(8,128)(2,1)S(1)} %bitcast.9), channel_id=1, source_target_pairs={{0,1},{1,0},{2,3},{3,2},{4,5},{5,4},{6,7},{7,6},{8,9},{9,8},{10,11... | collective-permute-start | bytes 1572872 | tf_op jit(solution)/shard_map/ppermute | solution.py:409
  62.6 3.5 %collective-permute-start.1 = (f32[16,40,128]{2,1,0:T(8,128)S(1)}, f32[16,40,128]{2,1,0:T(8,128)S(1)}, u32[]{:S(2)}, u32[]{:S(2)}) collective-permute-start(f32[16,40,128]{2,1,0:T(8,128)S(1)} %get-tuple-element.18), channel_id=1, source_target_pairs={{0,1},{1,0},{2,3},{3,2},{4,5},{5,4},{6,7},{7,6},{8,9},{9,8},{10,11... | collective-permute-start | bytes 983048 | tf_op jit(solution)/shard_map/ppermute | solution.py:411
